TPU v7x, 512 devices: a whole 4x4x16 slice. The times are simulated.
512 devices in a mesh: cells: 32 (over y, z_lo), snd: 16 (over x, z_hi, core).
Axes of the slice: x: 4, y: 4, z: 16 (z_hi: 2, z_lo: 8; z = z_hi * 8 + z_lo), core: 2. Of those that a mesh axis runs over, the one named last changes fastest.
Arguments:
- footprint: bfloat16 [128, 4, 12288], P(None, None, ('snd', 'cells')), may hold values from -24 to 24
- spatial_cov: bfloat16 [12288, 12288], P('snd', 'cells'), as said below
- week_scale: float32 [52], replicated, may hold values from 0.5 to 2
- band_width: int32 [1], replicated, may hold values from 2 to 8
- sounding_weeks: int32 [128], replicated, may hold values from 0 to 48
- target_print: bfloat16 [4096, 4, 12288], P('snd', None, 'cells'), may hold values from -0.0546875 to 0.0546875
- target_weeks: int32 [4096], P('snd'), may hold values from 0 to 48
Outputs:
- hq_rows: bfloat16 [128, 52, 12288], P('snd', None, 'cells')
- pair_cov: float32 [128, 4096], P(None, ('snd', 'cells'))
Inputs may be any that keep to these rules, and one draw needn't show every extreme that they name: spatial_cov is symmetric.
All inputs are finite; a program needn't handle non-finite values.
Results may differ from a plain program's by a relative error of at most 0.005.
Values may be sent and summed in bfloat16 or wider, within the bound.
A program may use at most 64 MiB of HBM per device.

v0:
```python
import jax
import jax.numpy as jnp
from jax import lax
from jax.sharding import PartitionSpec as P


def temporal_cov(week_scale, band_width):
    week_count = week_scale.shape[0]
    week_index = jnp.arange(week_count, dtype=jnp.int32)
    week_lag = jnp.abs(week_index[:, None] - week_index[None, :])
    in_band = (week_lag <= band_width[0]).astype(jnp.float32)
    decay = jnp.exp(-week_lag.astype(jnp.float32) / 6.0)
    return week_scale[:, None] * week_scale[None, :] * decay * in_band


def onehot_weeks(first_weeks, foot_len, week_count):
    foot_steps = jnp.arange(foot_len, dtype=jnp.int32)
    week_index = jnp.arange(week_count, dtype=jnp.int32)
    chosen = first_weeks[:, None, None] + foot_steps[None, :, None] == week_index[None, None, :]
    return chosen.astype(jnp.float32).reshape(first_weeks.shape[0] * foot_len, week_count)


def shards(
    footprint, spatial_cov, week_scale, band_width, sounding_weeks, target_print, target_weeks
):
    table = temporal_cov(week_scale, band_width)
    week_count = table.shape[0]
    column_block = lax.all_gather(footprint, "cells", axis=2, tiled=True)
    all_rows, foot_len = (column_block.shape[0], column_block.shape[1])
    own_rows = all_rows // lax.axis_size("snd")
    col_width = spatial_cov.shape[1]
    rows_mine = lax.all_to_all(
        column_block, "snd", split_axis=0, concat_axis=2, tiled=True
    ).reshape(own_rows * foot_len, -1)
    flux_map = jnp.dot(
        rows_mine,
        lax.all_gather(spatial_cov, "snd", axis=0, tiled=True),
        preferred_element_type=jnp.float32,
    )
    flux_bf = flux_map.astype(jnp.bfloat16).reshape(own_rows, foot_len, col_width)
    first_row = lax.axis_index("snd") * own_rows
    mine_weeks = lax.dynamic_slice_in_dim(sounding_weeks, first_row, own_rows, 0)
    spread = jnp.dot(
        onehot_weeks(mine_weeks, foot_len, week_count), table, precision=lax.Precision.HIGHEST
    ).reshape(own_rows, foot_len, week_count)
    hq_rows = jnp.einsum(
        "iaw,iac->iwc", spread, flux_bf.astype(jnp.float32), precision=lax.Precision.HIGHEST
    ).astype(jnp.bfloat16)
    target_count = target_print.shape[0]
    target_rows = jnp.transpose(target_print, (1, 0, 2)).reshape(foot_len * target_count, col_width)
    foot_steps = jnp.arange(foot_len, dtype=jnp.int32)
    week_index = jnp.arange(week_count, dtype=jnp.int32)
    target_pick = (
        target_weeks[None, :, None] + foot_steps[:, None, None] == week_index[None, None, :]
    )
    target_pick = target_pick.astype(jnp.float32).reshape(foot_len * target_count, week_count)
    shard_rows = lax.all_gather(flux_bf, "snd", axis=0, tiled=True)
    row_count = shard_rows.shape[0]
    row_table = jnp.dot(
        onehot_weeks(sounding_weeks, foot_len, week_count), table, precision=lax.Precision.HIGHEST
    )
    weights = lax.dot_general(
        row_table, target_pick, (((1,), (1,)), ((), ())), precision=lax.Precision.HIGHEST
    )
    products = lax.dot_general(
        shard_rows.reshape(row_count * foot_len, col_width),
        target_rows,
        (((1,), (1,)), ((), ())),
        preferred_element_type=jnp.float32,
    )
    partial_cov = (
        (weights * products).reshape(row_count, foot_len, foot_len, target_count).sum(axis=(1, 2))
    )
    pair_cov = lax.psum_scatter(partial_cov, "cells", scatter_dimension=1, tiled=True)
    return (hq_rows, pair_cov)


def solution(mesh):
    placed = (
        P(None, None, ("snd", "cells")),
        P("snd", "cells"),
        P(),
        P(),
        P(),
        P("snd", None, "cells"),
        P("snd"),
    )
    return jax.shard_map(
        shards,
        mesh=mesh,
        in_specs=placed,
        out_specs=(P("snd", None, "cells"), P(None, ("snd", "cells"))),
        check_vma=False,
    )
```

profile of v0, /device:TPU:1, one launch (start us, length us, event | category | flops | bytes accessed | tf_op | source)
XLA Modules:
  0.0 731.8 jit_solution(14179802652559674513)
XLA Ops:
  7.2 0.0 all-gather.2.cloned.1.call-start
  7.2 0.7 all-gather.2.cloned.1.call-update
  7.9 0.8 copy.14
  8.7 184.3 %all_gather.9 = bf16[128,4,768]{0,1,2:T(4,128)(2,1)S(1)} all-gather(bf16[128,4,24]{0,1,2:T(4,128)(2,1)S(1)} %copy.14), channel_id=1, replica_groups=mesh['cells'=32,'snd'=16] {'cells'}, dimensions={2}, use_global_device_ids=true | all-gather | bytes 811008 | tf_op jit(solution)/shard_map/all_gather | solution.py:28
  193.0 1.4 copy.15
  194.4 34.0 %all-to-all-start = ((bf16[128,4,768]{2,1,0:T(4,128)(2,1)}), bf16[128,4,768]{2,1,0:T(4,128)(2,1)S(1)}, u32[]{:S(2)}, u32[]{:S(2)}) async-start(bf16[128,4,768]{2,1,0:T(4,128)(2,1)} %copy.15), calls=%async_computation | async-start | bytes 1572864 | tf_op jit(solution)/shard_map/all_to_all | solution.py:32
  228.4 0.0 all-reduce.3.cloned.1.call-start
  229.1 0.1 dynamic_slice.3
  229.2 0.1 iota_add_fusion
  229.3 0.1 add.73
  229.4 1.0 copy.18
  230.4 1.3 dynamic-slice
  232.3 0.1 iota_add_fusion.1
  232.4 0.2 fusion.4
  232.6 0.4 fusion.2
  233.0 1.2 fusion
  234.3 31.9 %all-to-all-done = bf16[128,4,768]{2,1,0:T(4,128)(2,1)S(1)} async-done(((bf16[128,4,768]{2,1,0:T(4,128)(2,1)}), bf16[128,4,768]{2,1,0:T(4,128)(2,1)S(1)}, u32[]{:S(2)}, u32[]{:S(2)}) %all-to-all-start) | async-done | bytes 786464 | tf_op jit(solution)/shard_map/all_to_all | solution.py:32
  266.2 0.1 copy.24
  266.3 0.1 copy.17
  266.4 0.2 copy.21
  266.7 0.0 all-gather.2.cloned.1.call-done
  266.7 5.1 convolution_convert_fusion.1
  271.8 45.5 %all_gather.11 = bf16[128,4,384]{2,1,0:T(4,128)(2,1)S(1)} all-gather(bf16[8,4,384]{2,1,0:T(4,128)(2,1)S(1)} %reshape.111), channel_id=1, replica_groups=mesh['cells'=32,'snd'=16] {'snd'}, dimensions={0}, use_global_device_ids=true | all-gather | bytes 417792 | tf_op jit(solution)/shard_map/all_gather | solution.py:57
  317.4 0.1 reshape.112
  317.5 3.2 convolution_multiply_fusion
  320.7 2.2 reshape.114
  322.9 0.8 reduce_sum.9
  323.8 0.8 copy.19
  324.5 0.6 convolution_convert_fusion
  325.1 0.8 copy.20
  325.9 397.8 %all-reduce.3.cloned.1.call-done = f32[128,256]{0,1:T(8,128)} async-done(((f32[128,256]{0,1:T(8,128)}), f32[128,256]{0,1:T(8,128)}) %all-reduce.3.cloned.1.call-update) | async-done | bytes 131088
  723.7 1.3 constant_dynamic-slice_fusion
  (14 shorter events, 0.1 us)
Async XLA Ops:
  7.2 259.5 %all-gather.2.cloned.1.call-start = ((), (), s32[]{:S(2)}) async-start(), calls=%async_computation.1 | async-start | bytes 10027008 | tf_op jit(solution)/shard_map/all_gather | solution.py:37
  7.9 221.2 %copy-start.2 = (s32[128]{0:T(128)S(1)}, s32[128]{0:T(128)}, u32[]{:S(2)}) copy-start(s32[128]{0:T(128)} %param.11) | copy-start | bytes 1540
  7.9 221.5 %copy-start = (bf16[256,4,384]{2,1,0:T(4,128)(2,1)S(1)}, bf16[256,4,384]{2,1,0:T(4,128)(2,1)}, u32[]{:S(2)}) copy-start(bf16[256,4,384]{2,1,0:T(4,128)(2,1)} %param.12) | copy-start | bytes 2359300
  193.0 37.4 %copy-start.1 = (s32[256]{0:T(256)S(1)}, s32[256]{0:T(256)}, u32[]{:S(2)}) copy-start(s32[256]{0:T(256)} %param.13) | copy-start | bytes 3076
  193.0 39.4 %copy-start.3 = (f32[52]{0:T(128)S(1)}, f32[52]{0:T(128)}, u32[]{:S(2)}) copy-start(f32[52]{0:T(128)} %param.9) | copy-start | bytes 628
  194.4 71.8 %all-to-all-start = ((bf16[128,4,768]{2,1,0:T(4,128)(2,1)}), bf16[128,4,768]{2,1,0:T(4,128)(2,1)S(1)}, u32[]{:S(2)}, u32[]{:S(2)}) async-start(bf16[128,4,768]{2,1,0:T(4,128)(2,1)} %copy.15), calls=%async_computation | async-start | bytes 1572864 | tf_op jit(solution)/shard_map/all_to_all | solution.py:32
  228.4 495.3 %all-reduce.3.cloned.1.call-start = ((), (), s32[]{:S(2)}) async-start(), calls=%async_computation.2 | async-start | bytes 262144
Sparse Core Ops, SparseCore 0:
  11.3 211.4 all-gather.1
  324.7 398.9 all-reduce.2
where the time goes:
time: 746 us; the launch traced here: 732 us
  waiting for transfers between devices  430 us (58%)
  blocking collectives  230 us (31%)
  starting transfers between devices  34.1 us (5%)
  between operations  15.5 us (2%)
  matrix products  10.8 us (1%)
  local copies, waits for them, and re-layouts  10.2 us (1%)
    unnamed x3, waiting for transfers between devices  398 us
    all_gather x1, blocking collectives, shards(): column_block = lax.all_gather(footprint, 'cells', axis=2, tiled=True)  184 us
    all_gather x1, blocking collectives, shards(): shard_rows = lax.all_gather(flux_bf, 'snd', axis=0, tiled=True)  45.5 us
    all_to_all x1, starting transfers between devices, shards(): lax.all_to_all(column_block, 'snd', split_axis=0, concat_axis=2, tiled=True)  34 us
    all_to_all x1, waiting for transfers between devices, shards(): lax.all_to_all(column_block, 'snd', split_axis=0, concat_axis=2, tiled=True)  31.9 us
  transfers between devices with their start and end apart: 3, of which 2 were waited for; matrix products, arithmetic and copies ran while one was open for 1% of the time, Pallas kernels for 0%

commit v1 on v0

v1 whole, which is shorter than its diff:
```python
import functools

import jax
import jax.numpy as jnp
from jax import lax
from jax.experimental import pallas as pl
from jax.experimental.pallas import tpu as pltpu
from jax.sharding import PartitionSpec as P

MESH = pl.DeviceIdType.MESH
F32, BF16, I32 = jnp.float32, jnp.bfloat16, jnp.int32
X, Y, ZL = 4, 4, 8
CELLS, SND = 32, 16
KC = 24
COLS = 384
HALF = 256
SHARD = COLS // X
AWAY = (1, 3, 2)
BACK = (1, 0, 2)


def iota(shape, dim):
    return lax.broadcasted_iota(I32, shape, dim)


def dot_nt(a, b, precision=None):
    return lax.dot_general(
        a, b, (((1,), (1,)), ((), ())), precision=precision, preferred_element_type=F32
    )


def dot_nn(a, b, precision=None):
    return lax.dot_general(
        a, b, (((1,), (0,)), ((), ())), precision=precision, preferred_element_type=F32
    )


def flip_bits(pos, mask):
    out = 0
    for bit in (0, 1, 2):
        value = (pos // (1 << bit)) % 2
        out = out + (1 << bit) * (1 - value if mask & (1 << bit) else value)
    return out


def kernel(
    f_hbm, c_hbm, g_hbm, scale_hbm, band_ref, sw_hbm, tw_hbm,
    hq_ref, pc_ref,
    raw, c_buf, ct, g3, g2, scale_v, sw_v, tw_v,
    weights, spread, ft, acc, core_out, core_in, x_out, x_in, z_out, z_in,
    flux, pair_x, pair_out, pair_in,
    load_sem, zs_sem, zr_sem, ys_sem, yr_sem, cs_sem, cr_sem, xs_sem, xr_sem,
    hs_sem, hr_sem, gs_sem, gr_sem, fs_sem, fr_sem, ps_sem, pr_sem,
):
    cell = lax.axis_index("cells")
    snd = lax.axis_index("snd")
    x, zh, core = snd // 4, (snd // 2) % 2, snd % 2
    y, zl = cell // ZL, cell % ZL

    def at_cells(yy, zz):
        return (yy * ZL + zz, snd)

    def at_snd(xx, hh, cc):
        return (cell, (xx * 2 + hh) * 2 + cc)

    def remote(src, dst, send, recv, device):
        return pltpu.make_async_remote_copy(
            src_ref=src, dst_ref=dst, send_sem=send, recv_sem=recv,
            device_id=device, device_id_type=MESH,
        )

    z_peers = [flip_bits(zl, m) for m in range(1, ZL)]
    y_peers = [(y + d) % Y for d in AWAY]
    x_peers = [(x + d) % X for d in AWAY]
    opposite = at_snd(x, 1 - zh, core)
    sibling = at_snd(x, zh, 1 - core)

    barrier = pltpu.get_barrier_semaphore()
    greeted = [opposite]
    greeted += [at_cells(y, p) for p in z_peers[::-1]]
    greeted += [at_cells(p, zl) for p in y_peers]
    greeted += [at_snd(p, zh, core) for p in x_peers]
    greeted += [sibling]
    for device in greeted:
        pl.semaphore_signal(barrier, inc=1, device_id=device, device_id_type=MESH)

    load_f = pltpu.make_async_copy(f_hbm, raw.at[cell], load_sem.at[0])
    load_f.start()
    loads = [
        pltpu.make_async_copy(src, dst, load_sem.at[1 + n])
        for n, (src, dst) in enumerate(
            ((scale_hbm, scale_v), (sw_hbm, sw_v), (tw_hbm, tw_v), (c_hbm, c_buf), (g_hbm, g3))
        )
    ]
    for copy in loads:
        copy.start()
    load_f.wait()
    pl.semaphore_wait(barrier, len(greeted))

    for m, peer in enumerate(z_peers):
        remote(raw.at[cell], raw.at[cell], zs_sem, zr_sem.at[m], at_cells(y, peer)).start()
    for n, peer in enumerate(y_peers):
        remote(raw.at[cell], raw.at[cell], ys_sem, yr_sem.at[BACK[n]], at_cells(peer, zl)).start()

    def forward(m):
        block = raw.at[y * ZL + z_peers[m]]
        remote(block, block, zs_sem, zr_sem.at[m], opposite).wait_recv()
        for n, peer in enumerate(y_peers):
            remote(block, block, ys_sem, yr_sem.at[BACK[n]], at_cells(peer, zl)).start()

    for copy in loads[:3]:
        copy.wait()
    top = lax.Precision.HIGHEST
    scale8 = jnp.broadcast_to(scale_v[...], (8, 52))
    eye = (iota((64, 52), 0) == iota((64, 52), 1)).astype(F32)
    scale_row = dot_nt(scale8, eye, top)
    scale_col = dot_nt(eye, scale8, top)
    lag = jnp.abs(iota((64, 64), 0) - iota((64, 64), 1))
    decay = jnp.exp(lag.astype(F32) * (-1.0 / 6.0))
    table = jnp.where(lag <= band_ref[0], decay, 0.0)
    table = table * scale_col[:, 0:1] * scale_row[0:1, :]
    first = sw_v[...]
    weeks = jnp.concatenate([first + a for a in range(4)], axis=1)
    source_pick = (iota((64, 512), 0) == weeks).astype(F32)
    source_rows = dot_nn(table, source_pick, top)
    row_hi = source_rows.astype(BF16)
    rest = source_rows - row_hi.astype(F32)
    row_mid = rest.astype(BF16)
    row_lo = (rest - row_mid.astype(F32)).astype(BF16)
    rows3 = jnp.concatenate([row_hi, row_mid, row_lo], axis=0)
    repeat = ((iota((1024, 256), 0) >> 2) == iota((1024, 256), 1)).astype(BF16)
    target_first = jnp.broadcast_to(tw_v[...], (8, 256)).astype(F32).astype(BF16)
    target_col = dot_nt(repeat, target_first)[:, 0:1].astype(I32)
    target_week = target_col + (iota((1024, 1), 0) & 3)
    target_pick = ((iota((1024, 192), 1) & 63) == target_week).astype(F32).astype(BF16)
    forward(0)
    for h in range(2):
        weights[h] = dot_nn(target_pick, rows3[:, h * HALF : (h + 1) * HALF])
    forward(1)
    forward(2)
    mine = (iota((8, 512), 1) & 127) == iota((8, 512), 0) + snd * 8
    mine = mine.astype(F32)
    wide = (source_rows[:52].reshape(52, 1, 512) * mine.reshape(1, 8, 512)).reshape(416, 512)
    wide_hi = wide.astype(BF16)
    wide_lo = (wide - wide_hi.astype(F32)).astype(BF16)
    for h in range(2):
        spread[0, h] = wide_hi[:, h * HALF : (h + 1) * HALF]
        spread[1, h] = wide_lo[:, h * HALF : (h + 1) * HALF]
    forward(3)
    loads[3].wait()
    for q in range(Y):
        rows = KC * ZL
        ct[q] = c_buf[q * rows : (q + 1) * rows, :].astype(F32).T.astype(BF16)
    forward(4)
    forward(5)
    forward(6)
    loads[4].wait()
    g2[...] = g3[...].reshape(1024, COLS)

    def unpack(yy):
        blocks = raw[pl.ds(yy * ZL, ZL)].astype(F32)
        for a in range(4):
            part = blocks[:, a * KC : (a + 1) * KC, :].reshape(ZL * KC, 128).astype(BF16)
            ft[a // 2, :, (a % 2) * 128 : (a % 2 + 1) * 128] = part

    unpack(y)
    for h in range(2):
        acc[h] = dot_nn(ct[y], ft[h])
    for n, peer in enumerate(y_peers):
        part = raw.at[pl.ds(peer * ZL, ZL)]
        remote(part, part, ys_sem, yr_sem.at[n], opposite).wait_recv()
        unpack(peer)
        if n < 2:
            for h in range(2):
                acc[h] += dot_nn(ct[peer], ft[h])
        else:
            core_out[...] = (acc[1 - core] + dot_nn(ct[peer], ft[1 - core])).astype(BF16)
            to_core = remote(core_out, core_in, cs_sem, cr_sem, sibling)
            to_core.start()
            acc[core] += dot_nn(ct[peer], ft[core])

    to_core.wait_recv()
    chip_sum = acc[core] + core_in[...].astype(F32)
    acc[core] = chip_sum
    x_out[...] = chip_sum.astype(BF16).reshape(X, SHARD, HALF)
    x_copies = []
    for n, peer in enumerate(x_peers):
        copy = remote(x_out.at[peer], x_in.at[n], xs_sem, xr_sem, at_snd(peer, zh, core))
        copy.start()
        x_copies.append(copy)
    own = acc[core, pl.ds(pl.multiple_of(x * SHARD, SHARD), SHARD), :]
    remote(x_in, x_in, xs_sem, xr_sem, opposite).wait_recv()
    own = own + (x_in[0].astype(F32) + x_in[1].astype(F32) + x_in[2].astype(F32))
    z_out[...] = own.astype(BF16)
    to_z = remote(z_out, z_in, hs_sem, hr_sem, opposite)
    to_z.start()
    to_z.wait_recv()
    flux[core, x] = (own + z_in[...].astype(F32)).astype(BF16)

    def share(n, peer):
        block = flux.at[core, peer]
        remote(block, block, fs_sem, fr_sem, sibling).start()

    shard = flux.at[core, x]
    for n, peer in enumerate(x_peers):
        remote(shard, shard, gs_sem, gr_sem.at[BACK[n]], at_snd(peer, zh, core)).start()
    share(3, x)
    for n, peer in enumerate(x_peers):
        block = flux.at[core, peer]
        remote(block, block, gs_sem, gr_sem.at[n], opposite).wait_recv()
        share(n, peer)

    def products(h):
        both = dot_nn(g2[...], flux[h].reshape(COLS, HALF)) * weights[h]
        return both[:, :128] + both[:, 128:]

    pair_x[...] = products(core)
    whole = flux.at[1 - core]
    remote(whole, whole, fs_sem, fr_sem, sibling).wait_recv()
    total = pair_x[...] + products(1 - core)
    gather = ((iota((256, 1024), 1) >> 2) == iota((256, 1024), 0)).astype(BF16)
    total_hi = total.astype(BF16)
    total_lo = (total - total_hi.astype(F32)).astype(BF16)
    pair = dot_nn(gather, total_hi) + dot_nn(gather, total_lo)
    pair_out[...] = pair.reshape(CELLS, 8, 128)

    def send_pair(o, carry):
        target = (cell + o) % CELLS
        remote(
            pair_out.at[target], pair_in.at[o - 1], ps_sem, pr_sem, (target, snd)
        ).start()
        return carry

    lax.fori_loop(1, CELLS, send_pair, 0)

    hq = jnp.zeros((416, COLS), F32)
    for h in range(2):
        columns = flux[h].reshape(COLS, HALF)
        hq = hq + dot_nt(spread[0, h], columns) + dot_nt(spread[1, h], columns)
    hq_ref[...] = hq.astype(BF16)

    remote(pair_in, pair_in, ps_sem, pr_sem, opposite).wait_recv()
    pc_ref[...] = pair_out[cell] + jnp.sum(pair_in[...], axis=0)

    sent = raw.at[pl.ds(0, ZL - 1)]
    remote(sent, sent, zs_sem, zr_sem.at[0], opposite).wait_send()
    sent = raw.at[pl.ds(0, ZL * (Y - 1))]
    remote(sent, sent, ys_sem, yr_sem.at[0], opposite).wait_send()
    to_core.wait_send()
    remote(x_in, x_in, xs_sem, xr_sem, opposite).wait_send()
    to_z.wait_send()
    remote(x_in, x_in, gs_sem, gr_sem.at[0], opposite).wait_send()
    remote(x_out, x_out, fs_sem, fr_sem, sibling).wait_send()
    remote(pair_in, pair_in, ps_sem, pr_sem, opposite).wait_send()


def shards(
    footprint, spatial_cov, week_scale, band_width, sounding_weeks, target_print, target_weeks
):
    any_spec = pl.BlockSpec(memory_space=pl.ANY)
    vmem = pl.BlockSpec(memory_space=pltpu.VMEM)
    dma = pltpu.SemaphoreType.DMA
    hq, pair = pl.pallas_call(
        kernel,
        out_shape=(
            jax.ShapeDtypeStruct((416, COLS), BF16),
            jax.ShapeDtypeStruct((8, 128), F32),
        ),
        in_specs=[any_spec] * 4 + [pl.BlockSpec(memory_space=pltpu.SMEM)] + [any_spec] * 2,
        out_specs=(vmem, vmem),
        scratch_shapes=[
            pltpu.VMEM((CELLS, 4 * KC, 128), BF16),
            pltpu.VMEM((768, COLS), BF16),
            pltpu.VMEM((Y, COLS, KC * ZL), BF16),
            pltpu.VMEM((256, 4, COLS), BF16),
            pltpu.VMEM((1024, COLS), BF16),
            pltpu.VMEM((1, 52), F32),
            pltpu.VMEM((1, 128), I32),
            pltpu.VMEM((1, 256), I32),
            pltpu.VMEM((2, 1024, HALF), F32),
            pltpu.VMEM((2, 2, 416, HALF), BF16),
            pltpu.VMEM((2, KC * ZL, HALF), BF16),
            pltpu.VMEM((2, COLS, HALF), F32),
            pltpu.VMEM((COLS, HALF), BF16),
            pltpu.VMEM((COLS, HALF), BF16),
            pltpu.VMEM((X, SHARD, HALF), BF16),
            pltpu.VMEM((X - 1, SHARD, HALF), BF16),
            pltpu.VMEM((SHARD, HALF), BF16),
            pltpu.VMEM((SHARD, HALF), BF16),
            pltpu.VMEM((2, X, SHARD, HALF), BF16),
            pltpu.VMEM((1024, 128), F32),
            pltpu.VMEM((CELLS, 8, 128), F32),
            pltpu.VMEM((CELLS - 1, 8, 128), F32),
            dma((6,)),
            dma, dma((ZL - 1,)),
            dma, dma((Y - 1,)),
            dma, dma,
            dma, dma,
            dma, dma,
            dma, dma((X - 1,)),
            dma, dma,
            dma, dma,
        ],
        compiler_params=pltpu.CompilerParams(
            collective_id=0, has_side_effects=True, vmem_limit_bytes=48 << 20
        ),
        name="prior_products",
    )(
        jnp.transpose(footprint, (1, 2, 0)).reshape(4 * KC, 128),
        spatial_cov,
        target_print,
        week_scale.reshape(1, 52),
        band_width,
        sounding_weeks.reshape(1, 128),
        target_weeks.reshape(1, 256),
    )
    return jnp.transpose(hq.reshape(52, 8, COLS), (1, 0, 2)), pair.T


def solution(mesh):
    placed = (
        P(None, None, ("snd", "cells")),
        P("snd", "cells"),
        P(),
        P(),
        P(),
        P("snd", None, "cells"),
        P("snd"),
    )
    return jax.shard_map(
        shards,
        mesh=mesh,
        in_specs=placed,
        out_specs=(P("snd", None, "cells"), P(None, ("snd", "cells"))),
        check_vma=False,
    )
```

time: 746 us -> 67.1 us (0.09); the launches traced: 732 us -> 66.8 us
  waiting for transfers between devices: 430 us -> 0 us
  blocking collectives: 230 us -> 0 us
  Pallas kernels: 0 us -> 60.6 us
  starting transfers between devices: 34.1 us -> 0 us
  between operations: 15.5 us -> 1.31 us
  matrix products: 10.8 us -> 0 us
    unnamed x3 -> x0, waiting for transfers between devices: 398 us -> none
    all_gather x2 -> x0, blocking collectives: 230 us -> none  [the longest x1 184 us: shards(): column_block = lax.all_gather(footprint, 'cells', axis=2, tiled=True)]
    pallas_call x0 -> x1, Pallas kernels: none -> 60.6 us  [shards(): pl.pallas_call(kernel, out_shape=(jax.ShapeDtypeStruct((416, COLS), BF16)...]
    all_to_all x1 -> x0, starting transfers between devices: 34 us -> none  [shards(): lax.all_to_all(column_block, 'snd', split_axis=0, concat_axis=2, tiled=True)]
    all_to_all x1 -> x0, waiting for transfers between devices: 31.9 us -> none  [shards(): lax.all_to_all(column_block, 'snd', split_axis=0, concat_axis=2, tiled=True)]
    dot_general x6 -> x0, matrix products: 10.8 us -> none  [the longest x1 5.1 us: shards(): jnp.dot(rows_mine, lax.all_gather(spatial_cov, 'snd', axis=0, tiled=True)...]
  transfers between devices with their start and end apart: 3 -> 0, of which waited for: 2 -> 0; matrix products, arithmetic and copies ran while one was open for 1% -> 0% of each run, Pallas kernels for 0% -> 0%
where the time goes in v1:
time: 67.1 us; the launch traced here: 66.8 us
  Pallas kernels  60.6 us (90%)
  local copies, waits for them, and re-layouts  4.92 us (7%)
  between operations  1.31 us (2%)
    pallas_call x1, Pallas kernels, shards(): pl.pallas_call(kernel, out_shape=(jax.ShapeDtypeStruct((416, COLS), BF16)...  60.6 us
    unnamed x14, local copies, waits for them, and re-layouts  4.92 us

profile of v1, /device:TPU:1, one launch (start us, length us, event | category | flops | bytes accessed | tf_op | source)
XLA Modules:
  0.0 66.8 jit_solution(2146842898013972951)
XLA Ops:
  1.3 0.0 copy-start.5
  1.3 0.0 copy-start.3
  1.3 0.0 copy-start.4
  1.3 0.6 copy-done.5
  1.9 0.0 copy-done.3
  2.0 0.0 copy-done.4
  2.0 0.0 copy-start
  2.0 1.1 %copy-done = bf16[256,4,384]{2,1,0:T(4,128)(2,1)S(1)} copy-done((bf16[256,4,384]{2,1,0:T(4,128)(2,1)S(1)}, bf16[256,4,384]{2,1,0:T(4,128)(2,1)}, u32[]{:S(2)}) %copy-start) | copy-done | bytes 786456
  3.1 0.0 copy-start.1
  3.1 1.1 %copy-done.1 = bf16[768,384]{1,0:T(8,128)(2,1)S(1)} copy-done((bf16[768,384]{1,0:T(8,128)(2,1)S(1)}, bf16[768,384]{1,0:T(8,128)(2,1)}, u32[]{:S(2)}) %copy-start.1) | copy-done | bytes 589848
  4.2 0.0 copy-start.2
  4.2 0.7 %copy-done.2 = bf16[128,4,24]{0,2,1:T(8,128)(2,1)S(1)} copy-done((bf16[128,4,24]{0,2,1:T(8,128)(2,1)S(1)}, bf16[128,4,24]{0,2,1:T(8,128)(2,1)}, u32[]{:S(2)}) %copy-start.2) | copy-done | bytes 24600
  4.9 60.6 %prior_products.1 = (bf16[416,384]{1,0:T(8,128)(2,1)S(1)}, f32[8,128]{1,0:T(8,128)S(1)}) custom-call(bf16[96,128]{1,0:T(8,128)(2,1)S(1)} %bitcast.11, bf16[768,384]{1,0:T(8,128)(2,1)S(1)} %copy-done.1, bf16[256,4,384]{2,1,0:T(4,128)(2,1)S(1)} %copy-done, f32[1,52]{1,0:T(1,128)S(1)} %bitcast.14, s32[1]{0:T(128)S(6)} %copy.11.band_ref, s32[1,128]{1,0:T(1,128)S(1)} %bitcast.15, ...), custom_call_target="tpu_custom_call" | custom-call | tf_op jit(solution)/shard_map/prior_products/pallas_call | solution.py:263
  65.5 0.7 %copy.12 = bf16[8,52,384]{2,0,1:T(8,128)(2,1)} copy(bf16[8,52,384]{2,0,1:T(8,128)(2,1)S(1)} %bitcast.10) | data formatting | bytes 638976
  66.2 0.6 copy.13
Async XLA Ops:
  1.3 0.7 copy-start.5
  1.3 0.7 %copy-start.3 = (s32[256]{0:T(256)S(1)}, s32[256]{0:T(256)}, u32[]{:S(2)}) copy-start(s32[256]{0:T(256)} %param.13) | copy-start | bytes 3076
  1.3 0.7 %copy-start.4 = (f32[52]{0:T(128)S(1)}, f32[52]{0:T(128)}, u32[]{:S(2)}) copy-start(f32[52]{0:T(128)} %param.9) | copy-start | bytes 628
  2.0 1.1 %copy-start = (bf16[256,4,384]{2,1,0:T(4,128)(2,1)S(1)}, bf16[256,4,384]{2,1,0:T(4,128)(2,1)}, u32[]{:S(2)}) copy-start(bf16[256,4,384]{2,1,0:T(4,128)(2,1)} %g_hbm.1) | copy-start | bytes 2359300
  3.1 1.1 %copy-start.1 = (bf16[768,384]{1,0:T(8,128)(2,1)S(1)}, bf16[768,384]{1,0:T(8,128)(2,1)}, u32[]{:S(2)}) copy-start(bf16[768,384]{1,0:T(8,128)(2,1)} %c_hbm.1) | copy-start | bytes 1769476
  4.2 0.7 %copy-start.2 = (bf16[128,4,24]{0,2,1:T(8,128)(2,1)S(1)}, bf16[128,4,24]{0,2,1:T(8,128)(2,1)}, u32[]{:S(2)}) copy-start(bf16[128,4,24]{0,2,1:T(8,128)(2,1)} %param.7) | copy-start | bytes 73732

commit v2 on v1

--- a/solution.py
+++ b/solution.py
@@ -1,5 +1,3 @@
-import functools
-
 import jax
 import jax.numpy as jnp
 from jax import lax
@@ -69,6 +67,15 @@
             device_id=device, device_id_type=MESH,
         )
 
+    drains = []
+
+    def finish():
+        for drain in drains:
+            drain()
+
+    def later(ref, sem):
+        drains.append(remote(ref, ref, sem, load_sem.at[0], (cell, 15 - snd)).wait_send)
+
     z_peers = [flip_bits(zl, m) for m in range(1, ZL)]
     y_peers = [(y + d) % Y for d in AWAY]
     x_peers = [(x + d) % X for d in AWAY]
@@ -94,20 +101,6 @@
     ]
     for copy in loads:
         copy.start()
-    load_f.wait()
-    pl.semaphore_wait(barrier, len(greeted))
-
-    for m, peer in enumerate(z_peers):
-        remote(raw.at[cell], raw.at[cell], zs_sem, zr_sem.at[m], at_cells(y, peer)).start()
-    for n, peer in enumerate(y_peers):
-        remote(raw.at[cell], raw.at[cell], ys_sem, yr_sem.at[BACK[n]], at_cells(peer, zl)).start()
-
-    def forward(m):
-        block = raw.at[y * ZL + z_peers[m]]
-        remote(block, block, zs_sem, zr_sem.at[m], opposite).wait_recv()
-        for n, peer in enumerate(y_peers):
-            remote(block, block, ys_sem, yr_sem.at[BACK[n]], at_cells(peer, zl)).start()
-
     for copy in loads[:3]:
         copy.wait()
     top = lax.Precision.HIGHEST
@@ -133,11 +126,35 @@
     target_col = dot_nt(repeat, target_first)[:, 0:1].astype(I32)
     target_week = target_col + (iota((1024, 1), 0) & 3)
     target_pick = ((iota((1024, 192), 1) & 63) == target_week).astype(F32).astype(BF16)
-    forward(0)
     for h in range(2):
         weights[h] = dot_nn(target_pick, rows3[:, h * HALF : (h + 1) * HALF])
+    loads[3].wait()
+    for q in range(Y):
+        rows = KC * ZL
+        ct[q] = c_buf[q * rows : (q + 1) * rows, :].astype(F32).T.astype(BF16)
+    load_f.wait()
+    pl.semaphore_wait(barrier, len(greeted))
+
+    later(raw.at[pl.ds(0, ZL - 1)], zs_sem)
+    later(raw.at[pl.ds(0, ZL * (Y - 1))], ys_sem)
+    for m, peer in enumerate(z_peers):
+        remote(raw.at[cell], raw.at[cell], zs_sem, zr_sem.at[m], at_cells(y, peer)).start()
+    for n, peer in enumerate(y_peers):
+        remote(raw.at[cell], raw.at[cell], ys_sem, yr_sem.at[BACK[n]], at_cells(peer, zl)).start()
+
+    def forward(m):
+        block = raw.at[y * ZL + z_peers[m]]
+        remote(block, block, zs_sem, zr_sem.at[m], opposite).wait_recv()
+        for n, peer in enumerate(y_peers):
+            remote(block, block, ys_sem, yr_sem.at[BACK[n]], at_cells(peer, zl)).start()
+
+    forward(0)
     forward(1)
     forward(2)
+    forward(3)
+    forward(4)
+    forward(5)
+    forward(6)
     mine = (iota((8, 512), 1) & 127) == iota((8, 512), 0) + snd * 8
     mine = mine.astype(F32)
     wide = (source_rows[:52].reshape(52, 1, 512) * mine.reshape(1, 8, 512)).reshape(416, 512)
@@ -146,16 +163,9 @@
     for h in range(2):
         spread[0, h] = wide_hi[:, h * HALF : (h + 1) * HALF]
         spread[1, h] = wide_lo[:, h * HALF : (h + 1) * HALF]
-    forward(3)
-    loads[3].wait()
-    for q in range(Y):
-        rows = KC * ZL
-        ct[q] = c_buf[q * rows : (q + 1) * rows, :].astype(F32).T.astype(BF16)
-    forward(4)
-    forward(5)
-    forward(6)
     loads[4].wait()
     g2[...] = g3[...].reshape(1024, COLS)
+
 
     def unpack(yy):
         blocks = raw[pl.ds(yy * ZL, ZL)].astype(F32)
@@ -179,21 +189,21 @@
             to_core.start()
             acc[core] += dot_nn(ct[peer], ft[core])
 
+    drains.append(to_core.wait_send)
     to_core.wait_recv()
     chip_sum = acc[core] + core_in[...].astype(F32)
     acc[core] = chip_sum
     x_out[...] = chip_sum.astype(BF16).reshape(X, SHARD, HALF)
-    x_copies = []
+    later(x_in, xs_sem)
     for n, peer in enumerate(x_peers):
-        copy = remote(x_out.at[peer], x_in.at[n], xs_sem, xr_sem, at_snd(peer, zh, core))
-        copy.start()
-        x_copies.append(copy)
+        remote(x_out.at[peer], x_in.at[n], xs_sem, xr_sem, at_snd(peer, zh, core)).start()
     own = acc[core, pl.ds(pl.multiple_of(x * SHARD, SHARD), SHARD), :]
     remote(x_in, x_in, xs_sem, xr_sem, opposite).wait_recv()
     own = own + (x_in[0].astype(F32) + x_in[1].astype(F32) + x_in[2].astype(F32))
     z_out[...] = own.astype(BF16)
     to_z = remote(z_out, z_in, hs_sem, hr_sem, opposite)
     to_z.start()
+    drains.append(to_z.wait_send)
     to_z.wait_recv()
     flux[core, x] = (own + z_in[...].astype(F32)).astype(BF16)
 
@@ -202,6 +212,8 @@
         remote(block, block, fs_sem, fr_sem, sibling).start()
 
     shard = flux.at[core, x]
+    later(x_in, gs_sem)
+    later(x_out, fs_sem)
     for n, peer in enumerate(x_peers):
         remote(shard, shard, gs_sem, gr_sem.at[BACK[n]], at_snd(peer, zh, core)).start()
     share(3, x)
@@ -224,14 +236,14 @@
     pair = dot_nn(gather, total_hi) + dot_nn(gather, total_lo)
     pair_out[...] = pair.reshape(CELLS, 8, 128)
 
-    def send_pair(o, carry):
-        target = (cell + o) % CELLS
-        remote(
-            pair_out.at[target], pair_in.at[o - 1], ps_sem, pr_sem, (target, snd)
-        ).start()
-        return carry
-
-    lax.fori_loop(1, CELLS, send_pair, 0)
+    later(pair_in, ps_sem)
+    for m in range(ZL - 1, -1, -1):
+        for d in (2, 1, 3, 0):
+            if m or d:
+                target = ((y + d) % Y) * ZL + (z_peers[m - 1] if m else zl)
+                remote(
+                    pair_out.at[target], pair_in.at[m * Y + d - 1], ps_sem, pr_sem, (target, snd)
+                ).start()
 
     hq = jnp.zeros((416, COLS), F32)
     for h in range(2):
@@ -242,20 +254,11 @@
     remote(pair_in, pair_in, ps_sem, pr_sem, opposite).wait_recv()
     pc_ref[...] = pair_out[cell] + jnp.sum(pair_in[...], axis=0)
 
-    sent = raw.at[pl.ds(0, ZL - 1)]
-    remote(sent, sent, zs_sem, zr_sem.at[0], opposite).wait_send()
-    sent = raw.at[pl.ds(0, ZL * (Y - 1))]
-    remote(sent, sent, ys_sem, yr_sem.at[0], opposite).wait_send()
-    to_core.wait_send()
-    remote(x_in, x_in, xs_sem, xr_sem, opposite).wait_send()
-    to_z.wait_send()
-    remote(x_in, x_in, gs_sem, gr_sem.at[0], opposite).wait_send()
-    remote(x_out, x_out, fs_sem, fr_sem, sibling).wait_send()
-    remote(pair_in, pair_in, ps_sem, pr_sem, opposite).wait_send()
+    finish()
 
 
 def shards(
-    footprint, spatial_cov, week_scale, band_width, sounding_weeks, target_print, target_weeks
+    footprint, spatial_cov, week_scale, band_width, sounding_weeks, target_print, target_weeks,
 ):
     any_spec = pl.BlockSpec(memory_space=pl.ANY)
     vmem = pl.BlockSpec(memory_space=pltpu.VMEM)
@@ -302,7 +305,7 @@
             dma, dma,
         ],
         compiler_params=pltpu.CompilerParams(
-            collective_id=0, has_side_effects=True, vmem_limit_bytes=48 << 20
+            collective_id=0, has_side_effects=True, vmem_limit_bytes=62 << 20
         ),
         name="prior_products",
     )(

time: 67.1 us -> 64.9 us (0.967)
  local copies, waits for them, and re-layouts: 4.92 us -> 2.32 us
    unnamed x14 -> x4, local copies, waits for them, and re-layouts: 4.92 us -> 2.32 us
where the time goes in v2:
time: 64.9 us; the launch traced here: 64.7 us
  Pallas kernels  61.1 us (94%)
  local copies, waits for them, and re-layouts  2.32 us (4%)
  between operations  1.29 us (2%)
    pallas_call x1, Pallas kernels, shards(): pl.pallas_call(kernel, out_shape=(jax.ShapeDtypeStruct((416, COLS), BF16)...  61.1 us
    unnamed x4, local copies, waits for them, and re-layouts  2.32 us

profile of v2, /device:TPU:1, one launch (start us, length us, event | category | flops | bytes accessed | tf_op | source)
XLA Modules:
  0.0 64.7 jit_solution(556323658689106603)
XLA Ops:
  1.3 61.1 %prior_products.1 = (bf16[416,384]{1,0:T(8,128)(2,1)}, f32[8,128]{1,0:T(8,128)}) custom-call(bf16[96,128]{1,0:T(8,128)(2,1)} %bitcast.11, bf16[768,384]{1,0:T(8,128)(2,1)} %c_hbm.1, bf16[256,4,384]{2,1,0:T(4,128)(2,1)} %g_hbm.1, f32[1,52]{1,0:T(1,128)} %bitcast.14, s32[1]{0:T(128)S(6)} %copy.11.band_ref, s32[1,128]{1,0:T(1,128)} %bitcast.15, s32[1,256]{1,0:T(1,128)} %bitcast.13), custom_call_target="tpu_custom_call" | custom-call | tf_op jit(solution)/shard_map/prior_products/pallas_call | solution.py:266
  62.4 0.0 copy-start
  62.4 1.7 %copy.12 = bf16[8,52,384]{2,0,1:T(8,128)(2,1)} copy(bf16[8,52,384]{2,0,1:T(8,128)(2,1)} %bitcast.10) | data formatting | bytes 638976
  64.1 0.0 copy-done
  64.1 0.6 copy.13
Async XLA Ops:
  62.4 1.7 %copy-start = (f32[8,128]{1,0:T(8,128)S(1)}, f32[8,128]{1,0:T(8,128)}, u32[]{:S(2)}) copy-start(f32[8,128]{1,0:T(8,128)} %get-tuple-element.5) | copy-start | bytes 12292

commit v3 on v2

v3 whole, which is shorter than its diff:
```python
import jax
import jax.numpy as jnp
from jax import lax
from jax.experimental import pallas as pl
from jax.experimental.pallas import tpu as pltpu
from jax.sharding import PartitionSpec as P

MESH = pl.DeviceIdType.MESH
F32, BF16, I32 = jnp.float32, jnp.bfloat16, jnp.int32
X, Y, ZL = 4, 4, 8
CELLS = 32
KC = 24
COLS = 384
SHARD = COLS // X
CHUNKS = 2
ROWS = 2 * KC
GROUP = ZL * KC
AWAY = (1, 3, 2)
BACK = (1, 0, 2)
FAR_FIRST = (7, 6, 5, 4, 3, 2, 1)
NEAR_FIRST = (1, 2, 3, 4, 5, 6, 7)


def iota(shape, dim):
    return lax.broadcasted_iota(I32, shape, dim)


def dot_nt(a, b, precision=None):
    return lax.dot_general(
        a, b, (((1,), (1,)), ((), ())), precision=precision, preferred_element_type=F32
    )


def dot_nn(a, b, precision=None):
    return lax.dot_general(
        a, b, (((1,), (0,)), ((), ())), precision=precision, preferred_element_type=F32
    )


def flip_bits(pos, mask):
    out = 0
    for bit in (0, 1, 2):
        value = (pos // (1 << bit)) % 2
        out = out + (1 << bit) * (1 - value if mask & (1 << bit) else value)
    return out


def in_hbm(array):
    return pltpu.with_memory_space_constraint(array, pltpu.HBM)


def kernel(
    f_hbm, c_hbm, g_hbm, scale_hbm, band_ref, sw_hbm, tw_hbm,
    hq_ref, pc_ref,
    raw, c_buf, ct, g3, g2, scale_v, sw_v, tw_v,
    weights, spread, acc, sum_out, sum_in, z_out, z_in, z_own,
    flux, pair_x, pair_out, pair_in,
    load_sem, zs_sem, zr_sem, ys_sem, yr_sem, ss_sem, sr_sem,
    hs_sem, hr_sem, gs_sem, gr_sem, ps_sem, pr_sem, token,
):
    cell = lax.axis_index("cells")
    snd = lax.axis_index("snd")
    x, zh, core = snd // 4, (snd // 2) % 2, snd % 2
    y, zl = cell // ZL, cell % ZL

    def at_cells(yy, zz):
        return (yy * ZL + zz, snd)

    def at_snd(xx, hh, cc):
        return (cell, (xx * 2 + hh) * 2 + cc)

    def remote(src, dst, send, recv, device):
        return pltpu.make_async_remote_copy(
            src_ref=src, dst_ref=dst, send_sem=send, recv_sem=recv,
            device_id=device, device_id_type=MESH,
        )

    drains = []

    def finish():
        for drain in drains:
            drain()

    def later(ref, sem):
        drains.append(remote(ref, ref, sem, load_sem.at[0], opposite).wait_send)

    z_peer = {m: flip_bits(zl, m) for m in NEAR_FIRST}
    y_peers = [(y + d) % Y for d in AWAY]
    sum_peers = [
        ((x + d) % X, (core + f) % 2) for d in (2, 1, 3, 0) for f in (0, 1) if d or f
    ]
    opposite = at_snd(x, 1 - zh, core)
    across = (y * ZL + z_peer[4], (x * 2 + 1 - zh) * 2 + core)

    barrier = pltpu.get_barrier_semaphore()
    greeted = [at_cells(y, z_peer[m]) for m in FAR_FIRST] + [across]
    greeted += [at_cells(p, zl) for p in y_peers]
    greeted += [at_snd(xx, zh, cc) for xx, cc in sum_peers]
    for device in greeted:
        pl.semaphore_signal(barrier, inc=1, device_id=device, device_id_type=MESH)

    load_f = pltpu.make_async_copy(f_hbm, raw.at[cell], load_sem.at[0])
    load_f.start()
    loads = [
        pltpu.make_async_copy(src, dst, load_sem.at[1 + n])
        for n, (src, dst) in enumerate(
            ((scale_hbm, scale_v), (sw_hbm, sw_v), (tw_hbm, tw_v), (c_hbm, c_buf), (g_hbm, g3))
        )
    ]
    for copy in loads:
        copy.start()

    for copy in loads[:3]:
        copy.wait()
    top = lax.Precision.HIGHEST
    scale8 = jnp.broadcast_to(scale_v[...], (8, 52))
    eye = (iota((64, 52), 0) == iota((64, 52), 1)).astype(F32)
    scale_row = dot_nt(scale8, eye, top)
    scale_col = dot_nt(eye, scale8, top)
    lag = jnp.abs(iota((64, 64), 0) - iota((64, 64), 1))
    decay = jnp.exp(lag.astype(F32) * (-1.0 / 6.0))
    table = jnp.where(lag <= band_ref[0], decay, 0.0)
    table = table * scale_col[:, 0:1] * scale_row[0:1, :]
    first = sw_v[...]
    weeks = jnp.concatenate([first + a for a in range(4)], axis=1)
    source_pick = (iota((64, 512), 0) == weeks).astype(F32)
    source_rows = dot_nn(table, source_pick, top)
    row_hi = source_rows.astype(BF16)
    rest = source_rows - row_hi.astype(F32)
    row_mid = rest.astype(BF16)
    row_lo = (rest - row_mid.astype(F32)).astype(BF16)
    rows3 = jnp.concatenate([row_hi, row_mid, row_lo], axis=0)
    repeat = ((iota((1024, 256), 0) >> 2) == iota((1024, 256), 1)).astype(BF16)
    target_first = jnp.broadcast_to(tw_v[...], (8, 256)).astype(F32).astype(BF16)
    target_col = dot_nt(repeat, target_first)[:, 0:1].astype(I32)
    target_week = target_col + (iota((1024, 1), 0) & 3)
    target_pick = ((iota((1024, 192), 1) & 63) == target_week).astype(F32).astype(BF16)
    for q in range(CHUNKS):
        weights[q] = dot_nn(target_pick, rows3[:, q * 256 : (q + 1) * 256])
    loads[3].wait()
    for g in range(Y):
        ct[g] = c_buf[g * GROUP : (g + 1) * GROUP, :].astype(F32).T.astype(BF16)

    load_f.wait()
    pl.semaphore_wait(barrier, len(greeted))
    pl.semaphore_signal(token, inc=1, device_id=across, device_id_type=MESH)

    later(raw.at[pl.ds(0, ZL - 1)], zs_sem)
    later(raw.at[pl.ds(0, ZL * (Y - 1))], ys_sem)

    def piece(q, block):
        return raw.at[block, pl.ds(q * ROWS, ROWS)]

    def along_y(q, block):
        part = piece(q, block)
        for n, peer in enumerate(y_peers):
            remote(part, part, ys_sem, yr_sem.at[q, BACK[n]], at_cells(peer, zl)).start()

    for q in range(CHUNKS):
        part = piece(q, cell)
        for m in NEAR_FIRST:
            remote(
                part, part, zs_sem, zr_sem.at[q, m - 1], at_cells(y, z_peer[m])
            ).start()
        along_y(q, cell)
    for q in range(CHUNKS):
        for m in NEAR_FIRST:
            block = y * ZL + z_peer[m]
            part = piece(q, block)
            remote(part, part, zs_sem, zr_sem.at[q, m - 1], opposite).wait_recv()
            along_y(q, block)

    loads[4].wait()
    g2[...] = g3[...].reshape(1024, COLS)
    mine = (iota((8, 512), 1) & 127) == iota((8, 512), 0) + snd * 8
    mine = mine.astype(F32)
    wide = (source_rows[:52].reshape(52, 1, 512) * mine.reshape(1, 8, 512)).reshape(416, 512)
    wide_hi = wide.astype(BF16)
    wide_lo = (wide - wide_hi.astype(F32)).astype(BF16)
    for q in range(CHUNKS):
        spread[0, q] = wide_hi[:, q * 256 : (q + 1) * 256]
        spread[1, q] = wide_lo[:, q * 256 : (q + 1) * 256]

    def unpack(q, group):
        blocks = raw[pl.ds(group * ZL, ZL), q * ROWS : (q + 1) * ROWS].astype(F32)
        return jnp.concatenate(
            [
                blocks[:, a * KC : (a + 1) * KC, :].reshape(GROUP, 128).astype(BF16)
                for a in range(2)
            ],
            axis=1,
        )

    def partial_flux(q):
        total = dot_nn(ct[y], unpack(q, y))
        for n, peer in enumerate(y_peers):
            part = raw.at[pl.ds(peer * ZL, ZL), pl.ds(q * ROWS, ROWS)]
            remote(part, part, ys_sem, yr_sem.at[q, n], opposite).wait_recv()
            total = total + dot_nn(ct[peer], unpack(q, peer))
        for c in range(2):
            half = total[:, c * 128 : (c + 1) * 128]
            acc[q, c] = half
            sum_out[q, c] = half.astype(BF16).reshape(X, SHARD, 128)
        later(sum_in.at[q], ss_sem.at[q])
        for n, (xx, cc) in enumerate(sum_peers):
            remote(
                sum_out.at[q, cc, xx], sum_in.at[q, n], ss_sem.at[q], sr_sem.at[q],
                at_snd(xx, zh, cc),
            ).start()

    def across_z(q):
        every = sum_in.at[q]
        remote(every, every, ss_sem.at[q], sr_sem.at[q], opposite).wait_recv()
        own = acc[q, core, pl.ds(pl.multiple_of(x * SHARD, SHARD), SHARD), :]
        own = own + jnp.sum(sum_in[q].astype(F32), axis=0)
        z_own[q] = own
        z_out[q] = own.astype(BF16)
        copy = remote(z_out.at[q], z_in.at[q], hs_sem.at[q], hr_sem.at[q], opposite)
        copy.start()
        drains.append(copy.wait_send)
        return copy

    def share(q, copy):
        copy.wait_recv()
        flux[q, core, x] = (z_own[q] + z_in[q].astype(F32)).astype(BF16)
        shard = flux.at[q, core, x]
        later(sum_in.at[q], gs_sem.at[q])
        for xx, cc in sum_peers:
            remote(shard, shard, gs_sem.at[q], gr_sem.at[q], at_snd(xx, zh, cc)).start()

    def whole_flux(q):
        return jnp.concatenate([flux[q, c].reshape(COLS, 128) for c in range(2)], axis=1)

    def products(q):
        every = sum_in.at[q]
        remote(every, every, gs_sem.at[q], gr_sem.at[q], opposite).wait_recv()
        both = dot_nn(g2[...], whole_flux(q)) * weights[q]
        return both[:, :128] + both[:, 128:]

    for q in range(CHUNKS):
        partial_flux(q)
    pl.semaphore_wait(token, 1)
    moved = [across_z(q) for q in range(CHUNKS)]
    for q in range(CHUNKS):
        share(q, moved[q])

    pair_x[...] = products(0)
    total = pair_x[...] + products(1)
    gather = ((iota((256, 1024), 1) >> 2) == iota((256, 1024), 0)).astype(BF16)
    total_hi = total.astype(BF16)
    total_lo = (total - total_hi.astype(F32)).astype(BF16)
    pair = dot_nn(gather, total_hi) + dot_nn(gather, total_lo)
    pair_out[...] = pair.reshape(CELLS, 8, 128)

    later(pair_in, ps_sem)
    for m in FAR_FIRST + (0,):
        for d in (2, 1, 3, 0):
            if m or d:
                target = ((y + d) % Y) * ZL + (z_peer[m] if m else zl)
                remote(
                    pair_out.at[target], pair_in.at[m * Y + d - 1], ps_sem, pr_sem, (target, snd)
                ).start()

    hq = jnp.zeros((416, COLS), F32)
    for q in range(CHUNKS):
        columns = whole_flux(q)
        hq = hq + dot_nt(spread[0, q], columns) + dot_nt(spread[1, q], columns)
    hq_ref[...] = hq.astype(BF16)

    remote(pair_in, pair_in, ps_sem, pr_sem, opposite).wait_recv()
    pc_ref[...] = pair_out[cell] + jnp.sum(pair_in[...], axis=0)

    finish()


def shards(
    footprint, spatial_cov, week_scale, band_width, sounding_weeks, target_print, target_weeks,
):
    hbm = pl.BlockSpec(memory_space=pltpu.HBM)
    vmem = pl.BlockSpec(memory_space=pltpu.VMEM)
    dma = pltpu.SemaphoreType.DMA
    hq, pair = pl.pallas_call(
        kernel,
        out_shape=(
            jax.ShapeDtypeStruct((416, COLS), BF16),
            jax.ShapeDtypeStruct((8, 128), F32),
        ),
        in_specs=[hbm] * 4 + [pl.BlockSpec(memory_space=pltpu.SMEM)] + [hbm] * 2,
        out_specs=(vmem, vmem),
        scratch_shapes=[
            pltpu.VMEM((CELLS, 4 * KC, 128), BF16),
            pltpu.VMEM((768, COLS), BF16),
            pltpu.VMEM((Y, COLS, GROUP), BF16),
            pltpu.VMEM((256, 4, COLS), BF16),
            pltpu.VMEM((1024, COLS), BF16),
            pltpu.VMEM((1, 52), F32),
            pltpu.VMEM((1, 128), I32),
            pltpu.VMEM((1, 256), I32),
            pltpu.VMEM((CHUNKS, 1024, 256), F32),
            pltpu.VMEM((2, CHUNKS, 416, 256), BF16),
            pltpu.VMEM((CHUNKS, 2, COLS, 128), F32),
            pltpu.VMEM((CHUNKS, 2, X, SHARD, 128), BF16),
            pltpu.VMEM((CHUNKS, 2 * X - 1, SHARD, 128), BF16),
            pltpu.VMEM((CHUNKS, SHARD, 128), BF16),
            pltpu.VMEM((CHUNKS, SHARD, 128), BF16),
            pltpu.VMEM((CHUNKS, SHARD, 128), F32),
            pltpu.VMEM((CHUNKS, 2, X, SHARD, 128), BF16),
            pltpu.VMEM((1024, 128), F32),
            pltpu.VMEM((CELLS, 8, 128), F32),
            pltpu.VMEM((CELLS - 1, 8, 128), F32),
            dma((6,)),
            dma, dma((CHUNKS, ZL - 1)),
            dma, dma((CHUNKS, Y - 1)),
            dma((CHUNKS,)), dma((CHUNKS,)),
            dma((CHUNKS,)), dma((CHUNKS,)),
            dma((CHUNKS,)), dma((CHUNKS,)),
            dma, dma,
            pltpu.SemaphoreType.REGULAR,
        ],
        compiler_params=pltpu.CompilerParams(
            collective_id=0, has_side_effects=True, vmem_limit_bytes=48 << 20
        ),
        name="prior_products",
    )(
        in_hbm(jnp.transpose(footprint, (1, 2, 0)).reshape(4 * KC, 128)),
        in_hbm(spatial_cov),
        in_hbm(target_print),
        in_hbm(week_scale.reshape(1, 52)),
        band_width,
        in_hbm(sounding_weeks.reshape(1, 128)),
        in_hbm(target_weeks.reshape(1, 256)),
    )
    return jnp.transpose(hq.reshape(52, 8, COLS), (1, 0, 2)), pair.T


def solution(mesh):
    placed = (
        P(None, None, ("snd", "cells")),
        P("snd", "cells"),
        P(),
        P(),
        P(),
        P("snd", None, "cells"),
        P("snd"),
    )
    return jax.shard_map(
        shards,
        mesh=mesh,
        in_specs=placed,
        out_specs=(P("snd", None, "cells"), P(None, ("snd", "cells"))),
        check_vma=False,
    )
```

time: 64.9 us -> 60.3 us (0.929)
  Pallas kernels: 61.1 us -> 57.6 us
  local copies, waits for them, and re-layouts: 2.32 us -> 1.32 us
    pallas_call x1, Pallas kernels: 61.1 us -> 57.6 us  [shards(): pl.pallas_call(kernel, out_shape=(jax.ShapeDtypeStruct((416, COLS), BF16)...]
    unnamed x4 -> x2, local copies, waits for them, and re-layouts: 2.32 us -> 1.32 us
where the time goes in v3:
time: 60.3 us; the launch traced here: 60.2 us
  Pallas kernels  57.6 us (96%)
  local copies, waits for them, and re-layouts  1.32 us (2%)
  between operations  1.29 us (2%)
    pallas_call x1, Pallas kernels, shards(): pl.pallas_call(kernel, out_shape=(jax.ShapeDtypeStruct((416, COLS), BF16)...  57.6 us
    unnamed x2, local copies, waits for them, and re-layouts  1.32 us

profile of v3, /device:TPU:1, one launch (start us, length us, event | category | flops | bytes accessed | tf_op | source)
XLA Modules:
  0.0 60.2 jit_solution(16441679849221625336)
XLA Ops:
  1.3 57.6 %prior_products.1 = (bf16[416,384]{1,0:T(8,128)(2,1)S(1)}, f32[8,128]{1,0:T(8,128)S(1)}) custom-call(bf16[96,128]{1,0:T(8,128)(2,1)} %bitcast.12, bf16[768,384]{1,0:T(8,128)(2,1)} %c_hbm.1, bf16[256,4,384]{2,1,0:T(4,128)(2,1)} %g_hbm.1, f32[1,52]{1,0:T(1,128)} %bitcast.14, s32[1]{0:T(128)S(6)} %copy.11.band_ref, s32[1,128]{1,0:T(1,128)} %bitcast.15, ...), custom_call_target="tpu_custom_call" | custom-call | tf_op jit(solution)/shard_map/prior_products/pallas_call | solution.py:282
  58.9 0.7 %copy.12 = bf16[8,52,384]{2,0,1:T(8,128)(2,1)} copy(bf16[8,52,384]{2,0,1:T(8,128)(2,1)S(1)} %bitcast.10) | data formatting | bytes 638976
  59.6 0.6 copy.13

commit v4 on v3

--- a/solution.py
+++ b/solution.py
@@ -18,7 +18,7 @@
 AWAY = (1, 3, 2)
 BACK = (1, 0, 2)
 FAR_FIRST = (7, 6, 5, 4, 3, 2, 1)
-NEAR_FIRST = (1, 2, 3, 4, 5, 6, 7)
+HALF_LINE = (4, 3, 2, 1)
 
 
 def iota(shape, dim):
@@ -84,7 +84,7 @@
     def later(ref, sem):
         drains.append(remote(ref, ref, sem, load_sem.at[0], opposite).wait_send)
 
-    z_peer = {m: flip_bits(zl, m) for m in NEAR_FIRST}
+    z_peer = {m: flip_bits(zl, m) for m in FAR_FIRST}
     y_peers = [(y + d) % Y for d in AWAY]
     sum_peers = [
         ((x + d) % X, (core + f) % 2) for d in (2, 1, 3, 0) for f in (0, 1) if d or f
@@ -93,7 +93,7 @@
     across = (y * ZL + z_peer[4], (x * 2 + 1 - zh) * 2 + core)
 
     barrier = pltpu.get_barrier_semaphore()
-    greeted = [at_cells(y, z_peer[m]) for m in FAR_FIRST] + [across]
+    greeted = [at_cells(y, z_peer[m]) for m in HALF_LINE] + [across]
     greeted += [at_cells(p, zl) for p in y_peers]
     greeted += [at_snd(xx, zh, cc) for xx, cc in sum_peers]
     for device in greeted:
@@ -156,19 +156,34 @@
         for n, peer in enumerate(y_peers):
             remote(part, part, ys_sem, yr_sem.at[q, BACK[n]], at_cells(peer, zl)).start()
 
-    for q in range(CHUNKS):
-        part = piece(q, cell)
-        for m in NEAR_FIRST:
-            remote(
-                part, part, zs_sem, zr_sem.at[q, m - 1], at_cells(y, z_peer[m])
-            ).start()
+    def along_z(q, block, m, slot):
+        part = piece(q, block)
+        remote(
+            part, part, zs_sem, zr_sem.at[q, slot - 1], at_cells(y, z_peer[m])
+        ).start()
+
+    def from_z(q, m):
+        block = y * ZL + z_peer[m]
+        part = piece(q, block)
+        remote(part, part, zs_sem, zr_sem.at[q, m - 1], opposite).wait_recv()
+        return block
+
+    for q in range(CHUNKS):
+        along_z(q, cell, 4, 4)
+    for q in range(CHUNKS):
+        for m in (1, 2, 3):
+            along_z(q, cell, m, m)
         along_y(q, cell)
     for q in range(CHUNKS):
-        for m in NEAR_FIRST:
-            block = y * ZL + z_peer[m]
-            part = piece(q, block)
-            remote(part, part, zs_sem, zr_sem.at[q, m - 1], opposite).wait_recv()
+        for m in (1, 4, 2, 3):
+            block = from_z(q, m)
+            if m == 4:
+                for near in (1, 2, 3):
+                    along_z(q, block, near, near + 4)
             along_y(q, block)
+    for q in range(CHUNKS):
+        for m in (5, 6, 7):
+            along_y(q, from_z(q, m))
 
     loads[4].wait()
     g2[...] = g3[...].reshape(1024, COLS)
@@ -271,6 +286,17 @@
     pc_ref[...] = pair_out[cell] + jnp.sum(pair_in[...], axis=0)
 
     finish()
+
+
+def publish(hq_ref, pair_ref, hq_out, pair_out, sem):
+    copies = [
+        pltpu.make_async_copy(src, dst, sem.at[n])
+        for n, (src, dst) in enumerate(((hq_ref, hq_out), (pair_ref, pair_out)))
+    ]
+    for copy in copies:
+        copy.start()
+    for copy in copies:
+        copy.wait()
 
 
 def shards(
@@ -330,6 +356,17 @@
         in_hbm(sounding_weeks.reshape(1, 128)),
         in_hbm(target_weeks.reshape(1, 256)),
     )
+    hq, pair = pl.pallas_call(
+        publish,
+        out_shape=(
+            jax.ShapeDtypeStruct((416, COLS), BF16),
+            jax.ShapeDtypeStruct((8, 128), F32),
+        ),
+        in_specs=[vmem, vmem],
+        out_specs=(pl.BlockSpec(memory_space=pl.ANY), pl.BlockSpec(memory_space=pl.ANY)),
+        scratch_shapes=[dma((2,))],
+        name="publish",
+    )(hq, pair)
     return jnp.transpose(hq.reshape(52, 8, COLS), (1, 0, 2)), pair.T
 
 

time: 60.3 us -> 60.7 us (level)
    pallas_call x0 -> x1, Pallas kernels: none -> 1.71 us  [shards(): pl.pallas_call(publish, out_shape=(jax.ShapeDtypeStruct((416, COLS), BF16...]
    pallas_call x1, Pallas kernels: 57.6 us -> 56.2 us  [shards(): pl.pallas_call(kernel, out_shape=(jax.ShapeDtypeStruct((416, COLS), BF16)...]
    unnamed x2 -> x4, local copies, waits for them, and re-layouts: 1.32 us -> 1.29 us
where the time goes in v4:
time: 60.7 us; the launch traced here: 60.5 us
  Pallas kernels  58 us (96%)
  local copies, waits for them, and re-layouts  1.29 us (2%)
  between operations  1.29 us (2%)
    pallas_call x1, Pallas kernels, shards(): pl.pallas_call(kernel, out_shape=(jax.ShapeDtypeStruct((416, COLS), BF16)...  56.2 us
    pallas_call x1, Pallas kernels, shards(): pl.pallas_call(publish, out_shape=(jax.ShapeDtypeStruct((416, COLS), BF16...  1.71 us
    unnamed x4, local copies, waits for them, and re-layouts  1.29 us

profile of v4, /device:TPU:1, one launch (start us, length us, event | category | flops | bytes accessed | tf_op | source)
XLA Modules:
  0.0 60.5 jit_solution(15509325164914471663)
XLA Ops:
  1.3 56.2 %prior_products.1 = (bf16[416,384]{1,0:T(8,128)(2,1)S(1)}, f32[8,128]{1,0:T(8,128)S(1)}) custom-call(bf16[96,128]{1,0:T(8,128)(2,1)} %bitcast.10, bf16[768,384]{1,0:T(8,128)(2,1)} %c_hbm.1, bf16[256,4,384]{2,1,0:T(4,128)(2,1)} %g_hbm.1, f32[1,52]{1,0:T(1,128)} %bitcast.12, s32[1]{0:T(128)S(6)} %copy.9.band_ref, s32[1,128]{1,0:T(1,128)} %bitcast.13, ...), custom_call_target="tpu_custom_call" | custom-call | tf_op jit(solution)/shard_map/prior_products/pallas_call | solution.py:308
  57.5 0.0 copy-start
  57.5 0.7 %copy-done = bf16[416,384]{1,0:T(8,128)(2,1)} copy-done((bf16[416,384]{1,0:T(8,128)(2,1)}, bf16[416,384]{1,0:T(8,128)(2,1)S(1)}, u32[]{:S(2)}) %copy-start) | copy-done | bytes 319512
  58.2 0.0 copy-start.1
  58.3 0.6 copy-done.1
  58.8 1.7 %publish.1 = (bf16[416,384]{1,0:T(8,128)(2,1)}, f32[8,128]{1,0:T(8,128)}) custom-call(bf16[416,384]{1,0:T(8,128)(2,1)} %copy-done, f32[8,128]{1,0:T(8,128)} %copy-done.1), custom_call_target="tpu_custom_call" | custom-call | tf_op jit(solution)/shard_map/publish/pallas_call | solution.py:359
Async XLA Ops:
  57.5 0.7 %copy-start = (bf16[416,384]{1,0:T(8,128)(2,1)}, bf16[416,384]{1,0:T(8,128)(2,1)S(1)}, u32[]{:S(2)}) copy-start(bf16[416,384]{1,0:T(8,128)(2,1)S(1)} %get-tuple-element.6.hq_ref) | copy-start | bytes 958468
  58.2 0.6 copy-start.1

commit v5 on v4

--- a/solution.py
+++ b/solution.py
@@ -14,6 +14,8 @@
 SHARD = COLS // X
 CHUNKS = 2
 ROWS = 2 * KC
+HALF = SHARD // 2
+PIECES = [(q, h) for q in range(CHUNKS) for h in range(2)]
 GROUP = ZL * KC
 AWAY = (1, 3, 2)
 BACK = (1, 0, 2)
@@ -216,49 +218,54 @@
             half = total[:, c * 128 : (c + 1) * 128]
             acc[q, c] = half
             sum_out[q, c] = half.astype(BF16).reshape(X, SHARD, 128)
-        later(sum_in.at[q], ss_sem.at[q])
-        for n, (xx, cc) in enumerate(sum_peers):
-            remote(
-                sum_out.at[q, cc, xx], sum_in.at[q, n], ss_sem.at[q], sr_sem.at[q],
-                at_snd(xx, zh, cc),
-            ).start()
-
-    def across_z(q):
-        every = sum_in.at[q]
-        remote(every, every, ss_sem.at[q], sr_sem.at[q], opposite).wait_recv()
-        own = acc[q, core, pl.ds(pl.multiple_of(x * SHARD, SHARD), SHARD), :]
-        own = own + jnp.sum(sum_in[q].astype(F32), axis=0)
-        z_own[q] = own
-        z_out[q] = own.astype(BF16)
-        copy = remote(z_out.at[q], z_in.at[q], hs_sem.at[q], hr_sem.at[q], opposite)
+        for h in range(2):
+            p = 2 * q + h
+            later(sum_in.at[p], ss_sem.at[p])
+            for n, (xx, cc) in enumerate(sum_peers):
+                remote(
+                    sum_out.at[q, cc, xx, pl.ds(h * HALF, HALF)], sum_in.at[p, n],
+                    ss_sem.at[p], sr_sem.at[p], at_snd(xx, zh, cc),
+                ).start()
+
+    def across_z(q, h):
+        p = 2 * q + h
+        every = sum_in.at[p]
+        remote(every, every, ss_sem.at[p], sr_sem.at[p], opposite).wait_recv()
+        rows = pl.ds(pl.multiple_of(x * SHARD + h * HALF, HALF), HALF)
+        own = acc[q, core, rows, :] + jnp.sum(sum_in[p].astype(F32), axis=0)
+        z_own[p] = own
+        z_out[p] = own.astype(BF16)
+        copy = remote(z_out.at[p], z_in.at[p], hs_sem.at[p], hr_sem.at[p], opposite)
         copy.start()
         drains.append(copy.wait_send)
         return copy
 
-    def share(q, copy):
+    def share(q, h, copy):
+        p = 2 * q + h
         copy.wait_recv()
-        flux[q, core, x] = (z_own[q] + z_in[q].astype(F32)).astype(BF16)
-        shard = flux.at[q, core, x]
-        later(sum_in.at[q], gs_sem.at[q])
+        flux[q, core, x, h * HALF : (h + 1) * HALF] = (z_own[p] + z_in[p].astype(F32)).astype(BF16)
+        part = flux.at[q, core, x, pl.ds(h * HALF, HALF)]
+        later(sum_in.at[p], gs_sem.at[p])
         for xx, cc in sum_peers:
-            remote(shard, shard, gs_sem.at[q], gr_sem.at[q], at_snd(xx, zh, cc)).start()
+            remote(part, part, gs_sem.at[p], gr_sem.at[p], at_snd(xx, zh, cc)).start()
 
     def whole_flux(q):
         return jnp.concatenate([flux[q, c].reshape(COLS, 128) for c in range(2)], axis=1)
 
     def products(q):
-        every = sum_in.at[q]
-        remote(every, every, gs_sem.at[q], gr_sem.at[q], opposite).wait_recv()
+        for h in range(2):
+            p = 2 * q + h
+            every = sum_in.at[p]
+            remote(every, every, gs_sem.at[p], gr_sem.at[p], opposite).wait_recv()
         both = dot_nn(g2[...], whole_flux(q)) * weights[q]
         return both[:, :128] + both[:, 128:]
 
     for q in range(CHUNKS):
         partial_flux(q)
     pl.semaphore_wait(token, 1)
-    moved = [across_z(q) for q in range(CHUNKS)]
-    for q in range(CHUNKS):
-        share(q, moved[q])
-
+    moved = [across_z(q, h) for q, h in PIECES]
+    for q, h in PIECES:
+        share(q, h, moved[2 * q + h])
     pair_x[...] = products(0)
     total = pair_x[...] + products(1)
     gather = ((iota((256, 1024), 1) >> 2) == iota((256, 1024), 0)).astype(BF16)
@@ -286,17 +293,6 @@
     pc_ref[...] = pair_out[cell] + jnp.sum(pair_in[...], axis=0)
 
     finish()
-
-
-def publish(hq_ref, pair_ref, hq_out, pair_out, sem):
-    copies = [
-        pltpu.make_async_copy(src, dst, sem.at[n])
-        for n, (src, dst) in enumerate(((hq_ref, hq_out), (pair_ref, pair_out)))
-    ]
-    for copy in copies:
-        copy.start()
-    for copy in copies:
-        copy.wait()
 
 
 def shards(
@@ -326,10 +322,10 @@
             pltpu.VMEM((2, CHUNKS, 416, 256), BF16),
             pltpu.VMEM((CHUNKS, 2, COLS, 128), F32),
             pltpu.VMEM((CHUNKS, 2, X, SHARD, 128), BF16),
-            pltpu.VMEM((CHUNKS, 2 * X - 1, SHARD, 128), BF16),
-            pltpu.VMEM((CHUNKS, SHARD, 128), BF16),
-            pltpu.VMEM((CHUNKS, SHARD, 128), BF16),
-            pltpu.VMEM((CHUNKS, SHARD, 128), F32),
+            pltpu.VMEM((len(PIECES), 2 * X - 1, HALF, 128), BF16),
+            pltpu.VMEM((len(PIECES), HALF, 128), BF16),
+            pltpu.VMEM((len(PIECES), HALF, 128), BF16),
+            pltpu.VMEM((len(PIECES), HALF, 128), F32),
             pltpu.VMEM((CHUNKS, 2, X, SHARD, 128), BF16),
             pltpu.VMEM((1024, 128), F32),
             pltpu.VMEM((CELLS, 8, 128), F32),
@@ -337,9 +333,9 @@
             dma((6,)),
             dma, dma((CHUNKS, ZL - 1)),
             dma, dma((CHUNKS, Y - 1)),
-            dma((CHUNKS,)), dma((CHUNKS,)),
-            dma((CHUNKS,)), dma((CHUNKS,)),
-            dma((CHUNKS,)), dma((CHUNKS,)),
+            dma((len(PIECES),)), dma((len(PIECES),)),
+            dma((len(PIECES),)), dma((len(PIECES),)),
+            dma((len(PIECES),)), dma((len(PIECES),)),
             dma, dma,
             pltpu.SemaphoreType.REGULAR,
         ],
@@ -356,17 +352,6 @@
         in_hbm(sounding_weeks.reshape(1, 128)),
         in_hbm(target_weeks.reshape(1, 256)),
     )
-    hq, pair = pl.pallas_call(
-        publish,
-        out_shape=(
-            jax.ShapeDtypeStruct((416, COLS), BF16),
-            jax.ShapeDtypeStruct((8, 128), F32),
-        ),
-        in_specs=[vmem, vmem],
-        out_specs=(pl.BlockSpec(memory_space=pl.ANY), pl.BlockSpec(memory_space=pl.ANY)),
-        scratch_shapes=[dma((2,))],
-        name="publish",
-    )(hq, pair)
     return jnp.transpose(hq.reshape(52, 8, COLS), (1, 0, 2)), pair.T
 
 

time: 60.7 us -> 57.7 us (0.951)
  Pallas kernels: 58 us -> 55 us
    pallas_call x1 -> x0, Pallas kernels: 1.71 us -> none  [shards(): pl.pallas_call(publish, out_shape=(jax.ShapeDtypeStruct((416, COLS), BF16...]
    pallas_call x1, Pallas kernels: 56.2 us -> 55 us  [shards(): pl.pallas_call(kernel, out_shape=(jax.ShapeDtypeStruct((416, COLS), BF16)...]
    unnamed x4 -> x2, local copies, waits for them, and re-layouts: 1.29 us -> 1.32 us
where the time goes in v5:
time: 57.7 us; the launch traced here: 57.6 us
  Pallas kernels  55 us (95%)
  local copies, waits for them, and re-layouts  1.32 us (2%)
  between operations  1.29 us (2%)
    pallas_call x1, Pallas kernels, shards(): pl.pallas_call(kernel, out_shape=(jax.ShapeDtypeStruct((416, COLS), BF16)...  55 us
    unnamed x2, local copies, waits for them, and re-layouts  1.32 us

profile of v5, /device:TPU:1, one launch (start us, length us, event | category | flops | bytes accessed | tf_op | source)
XLA Modules:
  0.0 57.6 jit_solution(14359749239893533000)
XLA Ops:
  1.3 55.0 %prior_products.1 = (bf16[416,384]{1,0:T(8,128)(2,1)S(1)}, f32[8,128]{1,0:T(8,128)S(1)}) custom-call(bf16[96,128]{1,0:T(8,128)(2,1)} %bitcast.12, bf16[768,384]{1,0:T(8,128)(2,1)} %c_hbm.1, bf16[256,4,384]{2,1,0:T(4,128)(2,1)} %g_hbm.1, f32[1,52]{1,0:T(1,128)} %bitcast.14, s32[1]{0:T(128)S(6)} %copy.11.band_ref, s32[1,128]{1,0:T(1,128)} %bitcast.15, ...), custom_call_target="tpu_custom_call" | custom-call | tf_op jit(solution)/shard_map/prior_products/pallas_call | solution.py:304
  56.3 0.7 %copy.12 = bf16[8,52,384]{2,0,1:T(8,128)(2,1)} copy(bf16[8,52,384]{2,0,1:T(8,128)(2,1)S(1)} %bitcast.10) | data formatting | bytes 638976
  57.0 0.6 %copy.13 = f32[128,8]{0,1:T(8,128)} copy(f32[128,8]{0,1:T(8,128)S(1)} %bitcast.11) | data formatting | bytes 8192

commit v6 on v5

--- a/solution.py
+++ b/solution.py
@@ -16,9 +16,10 @@
 ROWS = 2 * KC
 HALF = SHARD // 2
 PIECES = [(q, h) for q in range(CHUNKS) for h in range(2)]
-GROUP = ZL * KC
+QUAD = ZL // 2
+GROUP = Y * QUAD * KC
+TARGETS = 256
 AWAY = (1, 3, 2)
-BACK = (1, 0, 2)
 FAR_FIRST = (7, 6, 5, 4, 3, 2, 1)
 HALF_LINE = (4, 3, 2, 1)
 
@@ -132,16 +133,20 @@
     row_mid = rest.astype(BF16)
     row_lo = (rest - row_mid.astype(F32)).astype(BF16)
     rows3 = jnp.concatenate([row_hi, row_mid, row_lo], axis=0)
-    repeat = ((iota((1024, 256), 0) >> 2) == iota((1024, 256), 1)).astype(BF16)
+    repeat = ((iota((1024, 256), 0) & 255) == iota((1024, 256), 1)).astype(BF16)
     target_first = jnp.broadcast_to(tw_v[...], (8, 256)).astype(F32).astype(BF16)
     target_col = dot_nt(repeat, target_first)[:, 0:1].astype(I32)
-    target_week = target_col + (iota((1024, 1), 0) & 3)
+    target_week = target_col + (iota((1024, 1), 0) >> 8)
     target_pick = ((iota((1024, 192), 1) & 63) == target_week).astype(F32).astype(BF16)
     for q in range(CHUNKS):
         weights[q] = dot_nn(target_pick, rows3[:, q * 256 : (q + 1) * 256])
     loads[3].wait()
-    for g in range(Y):
-        ct[g] = c_buf[g * GROUP : (g + 1) * GROUP, :].astype(F32).T.astype(BF16)
+    for quad in range(2):
+        rows = [
+            c_buf[(g * 2 + quad) * QUAD * KC : (g * 2 + quad + 1) * QUAD * KC, :].astype(F32)
+            for g in range(Y)
+        ]
+        ct[quad] = jnp.concatenate(rows, axis=0).T.astype(BF16)
 
     load_f.wait()
     pl.semaphore_wait(barrier, len(greeted))
@@ -153,10 +158,10 @@
     def piece(q, block):
         return raw.at[block, pl.ds(q * ROWS, ROWS)]
 
-    def along_y(q, block):
+    def along_y(q, block, far):
         part = piece(q, block)
-        for n, peer in enumerate(y_peers):
-            remote(part, part, ys_sem, yr_sem.at[q, BACK[n]], at_cells(peer, zl)).start()
+        for peer in y_peers:
+            remote(part, part, ys_sem, yr_sem.at[q, far], at_cells(peer, zl)).start()
 
     def along_z(q, block, m, slot):
         part = piece(q, block)
@@ -175,20 +180,27 @@
     for q in range(CHUNKS):
         for m in (1, 2, 3):
             along_z(q, cell, m, m)
-        along_y(q, cell)
+        along_y(q, cell, 0)
+
+    loads[4].wait()
+    targets = g3[...].reshape(4 * TARGETS, COLS)
+    offset = iota((TARGETS, 4 * TARGETS), 1) - 4 * iota((TARGETS, 4 * TARGETS), 0)
+    for k in range(4):
+        g2[k * TARGETS : (k + 1) * TARGETS] = dot_nn(
+            (offset == k).astype(F32).astype(BF16), targets
+        ).astype(BF16)
+
     for q in range(CHUNKS):
         for m in (1, 4, 2, 3):
             block = from_z(q, m)
             if m == 4:
                 for near in (1, 2, 3):
                     along_z(q, block, near, near + 4)
-            along_y(q, block)
+            along_y(q, block, m // 4)
     for q in range(CHUNKS):
         for m in (5, 6, 7):
-            along_y(q, from_z(q, m))
-
-    loads[4].wait()
-    g2[...] = g3[...].reshape(1024, COLS)
+            along_y(q, from_z(q, m), 1)
+
     mine = (iota((8, 512), 1) & 127) == iota((8, 512), 0) + snd * 8
     mine = mine.astype(F32)
     wide = (source_rows[:52].reshape(52, 1, 512) * mine.reshape(1, 8, 512)).reshape(416, 512)
@@ -198,22 +210,35 @@
         spread[0, q] = wide_hi[:, q * 256 : (q + 1) * 256]
         spread[1, q] = wide_lo[:, q * 256 : (q + 1) * 256]
 
-    def unpack(q, group):
-        blocks = raw[pl.ds(group * ZL, ZL), q * ROWS : (q + 1) * ROWS].astype(F32)
-        return jnp.concatenate(
-            [
-                blocks[:, a * KC : (a + 1) * KC, :].reshape(GROUP, 128).astype(BF16)
-                for a in range(2)
-            ],
-            axis=1,
-        )
+    def unpack(q, quad):
+        blocks = [
+            raw[pl.ds((g * 2 + quad) * QUAD, QUAD), q * ROWS : (q + 1) * ROWS].astype(F32)
+            for g in range(Y)
+        ]
+        halves = [
+            jnp.concatenate(
+                [b[:, a * KC : (a + 1) * KC, :].reshape(QUAD * KC, 128) for b in blocks], axis=0
+            ).astype(BF16)
+            for a in range(2)
+        ]
+        return jnp.concatenate(halves, axis=1)
+
+    own_quad = zl // QUAD
+
+    def from_y(q, far):
+        part = raw.at[pl.ds(0, QUAD * (Y - 1)), pl.ds(0, ROWS)]
+        remote(part, part, ys_sem, yr_sem.at[q, far], opposite).wait_recv()
+
+    def near_flux(q):
+        from_y(q, 0)
+        total = dot_nn(ct[own_quad], unpack(q, own_quad))
+        for c in range(2):
+            acc[q, c] = total[:, c * 128 : (c + 1) * 128]
 
     def partial_flux(q):
-        total = dot_nn(ct[y], unpack(q, y))
-        for n, peer in enumerate(y_peers):
-            part = raw.at[pl.ds(peer * ZL, ZL), pl.ds(q * ROWS, ROWS)]
-            remote(part, part, ys_sem, yr_sem.at[q, n], opposite).wait_recv()
-            total = total + dot_nn(ct[peer], unpack(q, peer))
+        from_y(q, 1)
+        total = jnp.concatenate([acc[q, 0], acc[q, 1]], axis=1)
+        total = total + dot_nn(ct[1 - own_quad], unpack(q, 1 - own_quad))
         for c in range(2):
             half = total[:, c * 128 : (c + 1) * 128]
             acc[q, c] = half
@@ -258,8 +283,11 @@
             every = sum_in.at[p]
             remote(every, every, gs_sem.at[p], gr_sem.at[p], opposite).wait_recv()
         both = dot_nn(g2[...], whole_flux(q)) * weights[q]
-        return both[:, :128] + both[:, 128:]
-
+        both = both[:, :128] + both[:, 128:]
+        return jnp.sum(both.reshape(4, TARGETS, 128), axis=0)
+
+    for q in range(CHUNKS):
+        near_flux(q)
     for q in range(CHUNKS):
         partial_flux(q)
     pl.semaphore_wait(token, 1)
@@ -267,16 +295,13 @@
     for q, h in PIECES:
         share(q, h, moved[2 * q + h])
     pair_x[...] = products(0)
-    total = pair_x[...] + products(1)
-    gather = ((iota((256, 1024), 1) >> 2) == iota((256, 1024), 0)).astype(BF16)
-    total_hi = total.astype(BF16)
-    total_lo = (total - total_hi.astype(F32)).astype(BF16)
-    pair = dot_nn(gather, total_hi) + dot_nn(gather, total_lo)
-    pair_out[...] = pair.reshape(CELLS, 8, 128)
+    total = (pair_x[...] + products(1)).reshape(CELLS, 8, 128)
+    pair_x[...] = total.reshape(TARGETS, 128)
+    pair_out[...] = total.astype(BF16)
 
     later(pair_in, ps_sem)
-    for m in FAR_FIRST + (0,):
-        for d in (2, 1, 3, 0):
+    for d in (2, 1, 3, 0):
+        for m in FAR_FIRST + (0,):
             if m or d:
                 target = ((y + d) % Y) * ZL + (z_peer[m] if m else zl)
                 remote(
@@ -290,7 +315,8 @@
     hq_ref[...] = hq.astype(BF16)
 
     remote(pair_in, pair_in, ps_sem, pr_sem, opposite).wait_recv()
-    pc_ref[...] = pair_out[cell] + jnp.sum(pair_in[...], axis=0)
+    own = pair_x[pl.ds(pl.multiple_of(cell * 8, 8), 8), :]
+    pc_ref[...] = own + jnp.sum(pair_in[...].astype(F32), axis=0)
 
     finish()
 
@@ -312,7 +338,7 @@
         scratch_shapes=[
             pltpu.VMEM((CELLS, 4 * KC, 128), BF16),
             pltpu.VMEM((768, COLS), BF16),
-            pltpu.VMEM((Y, COLS, GROUP), BF16),
+            pltpu.VMEM((2, COLS, GROUP), BF16),
             pltpu.VMEM((256, 4, COLS), BF16),
             pltpu.VMEM((1024, COLS), BF16),
             pltpu.VMEM((1, 52), F32),
@@ -327,12 +353,12 @@
             pltpu.VMEM((len(PIECES), HALF, 128), BF16),
             pltpu.VMEM((len(PIECES), HALF, 128), F32),
             pltpu.VMEM((CHUNKS, 2, X, SHARD, 128), BF16),
-            pltpu.VMEM((1024, 128), F32),
-            pltpu.VMEM((CELLS, 8, 128), F32),
-            pltpu.VMEM((CELLS - 1, 8, 128), F32),
+            pltpu.VMEM((TARGETS, 128), F32),
+            pltpu.VMEM((CELLS, 8, 128), BF16),
+            pltpu.VMEM((CELLS - 1, 8, 128), BF16),
             dma((6,)),
             dma, dma((CHUNKS, ZL - 1)),
-            dma, dma((CHUNKS, Y - 1)),
+            dma, dma((CHUNKS, 2)),
             dma((len(PIECES),)), dma((len(PIECES),)),
             dma((len(PIECES),)), dma((len(PIECES),)),
             dma((len(PIECES),)), dma((len(PIECES),)),

time: 57.7 us -> 55.5 us (0.962)
  Pallas kernels: 55 us -> 52.7 us
    pallas_call x1, Pallas kernels: 55 us -> 52.7 us  [shards(): pl.pallas_call(kernel, out_shape=(jax.ShapeDtypeStruct((416, COLS), BF16)...]
where the time goes in v6:
time: 55.5 us; the launch traced here: 55.3 us
  Pallas kernels  52.7 us (95%)
  local copies, waits for them, and re-layouts  1.32 us (2%)
  between operations  1.29 us (2%)
    pallas_call x1, Pallas kernels, shards(): pl.pallas_call(kernel, out_shape=(jax.ShapeDtypeStruct((416, COLS), BF16)...  52.7 us
    unnamed x2, local copies, waits for them, and re-layouts  1.32 us

profile of v6, /device:TPU:1, one launch (start us, length us, event | category | flops | bytes accessed | tf_op | source)
XLA Modules:
  0.0 55.3 jit_solution(14740822584857771258)
XLA Ops:
  1.3 52.7 %prior_products.1 = (bf16[416,384]{1,0:T(8,128)(2,1)S(1)}, f32[8,128]{1,0:T(8,128)S(1)}) custom-call(bf16[96,128]{1,0:T(8,128)(2,1)} %bitcast.12, bf16[768,384]{1,0:T(8,128)(2,1)} %c_hbm.1, bf16[256,4,384]{2,1,0:T(4,128)(2,1)} %g_hbm.1, f32[1,52]{1,0:T(1,128)} %bitcast.14, s32[1]{0:T(128)S(6)} %copy.11.band_ref, s32[1,128]{1,0:T(1,128)} %bitcast.15, ...), custom_call_target="tpu_custom_call" | custom-call | tf_op jit(solution)/shard_map/prior_products/pallas_call | solution.py:330
  54.0 0.7 %copy.12 = bf16[8,52,384]{2,0,1:T(8,128)(2,1)} copy(bf16[8,52,384]{2,0,1:T(8,128)(2,1)S(1)} %bitcast.10) | data formatting | bytes 638976
  54.8 0.6 %copy.13 = f32[128,8]{0,1:T(8,128)} copy(f32[128,8]{0,1:T(8,128)S(1)} %bitcast.11) | data formatting | bytes 8192

commit v7 on v6

--- a/solution.py
+++ b/solution.py
@@ -53,9 +53,9 @@
 
 
 def kernel(
-    f_hbm, c_hbm, g_hbm, scale_hbm, band_ref, sw_hbm, tw_hbm,
+    f_hbm, c_hbm, g_hbm, scale_hbm, band_hbm, sw_hbm, tw_hbm,
     hq_ref, pc_ref,
-    raw, c_buf, ct, g3, g2, scale_v, sw_v, tw_v,
+    raw, c_buf, ct, g3, g2, scale_v, sw_v, tw_v, band_s,
     weights, spread, acc, sum_out, sum_in, z_out, z_in, z_own,
     flux, pair_x, pair_out, pair_in,
     load_sem, zs_sem, zr_sem, ys_sem, yr_sem, ss_sem, sr_sem,
@@ -107,13 +107,50 @@
     loads = [
         pltpu.make_async_copy(src, dst, load_sem.at[1 + n])
         for n, (src, dst) in enumerate(
-            ((scale_hbm, scale_v), (sw_hbm, sw_v), (tw_hbm, tw_v), (c_hbm, c_buf), (g_hbm, g3))
+            (
+                (scale_hbm, scale_v), (sw_hbm, sw_v), (tw_hbm, tw_v), (band_hbm, band_s),
+                (c_hbm, c_buf), (g_hbm, g3),
+            )
         )
     ]
     for copy in loads:
         copy.start()
 
-    for copy in loads[:3]:
+    load_f.wait()
+    pl.semaphore_wait(barrier, len(greeted))
+    pl.semaphore_signal(token, inc=1, device_id=across, device_id_type=MESH)
+
+    later(raw.at[pl.ds(0, ZL - 1)], zs_sem)
+    later(raw.at[pl.ds(0, ZL * (Y - 1))], ys_sem)
+
+    def piece(q, block):
+        return raw.at[block, pl.ds(q * ROWS, ROWS)]
+
+    def along_y(q, block, far):
+        part = piece(q, block)
+        for peer in y_peers:
+            remote(part, part, ys_sem, yr_sem.at[q, far], at_cells(peer, zl)).start()
+
+    def along_z(q, block, m, slot):
+        part = piece(q, block)
+        remote(
+            part, part, zs_sem, zr_sem.at[q, slot - 1], at_cells(y, z_peer[m])
+        ).start()
+
+    def from_z(q, m):
+        block = y * ZL + z_peer[m]
+        part = piece(q, block)
+        remote(part, part, zs_sem, zr_sem.at[q, m - 1], opposite).wait_recv()
+        return block
+
+    for q in range(CHUNKS):
+        along_z(q, cell, 4, 4)
+    for q in range(CHUNKS):
+        for m in (1, 2, 3):
+            along_z(q, cell, m, m)
+        along_y(q, cell, 0)
+
+    for copy in loads[:4]:
         copy.wait()
     top = lax.Precision.HIGHEST
     scale8 = jnp.broadcast_to(scale_v[...], (8, 52))
@@ -122,7 +159,7 @@
     scale_col = dot_nt(eye, scale8, top)
     lag = jnp.abs(iota((64, 64), 0) - iota((64, 64), 1))
     decay = jnp.exp(lag.astype(F32) * (-1.0 / 6.0))
-    table = jnp.where(lag <= band_ref[0], decay, 0.0)
+    table = jnp.where(lag <= band_s[0, 0], decay, 0.0)
     table = table * scale_col[:, 0:1] * scale_row[0:1, :]
     first = sw_v[...]
     weeks = jnp.concatenate([first + a for a in range(4)], axis=1)
@@ -140,7 +177,7 @@
     target_pick = ((iota((1024, 192), 1) & 63) == target_week).astype(F32).astype(BF16)
     for q in range(CHUNKS):
         weights[q] = dot_nn(target_pick, rows3[:, q * 256 : (q + 1) * 256])
-    loads[3].wait()
+    loads[4].wait()
     for quad in range(2):
         rows = [
             c_buf[(g * 2 + quad) * QUAD * KC : (g * 2 + quad + 1) * QUAD * KC, :].astype(F32)
@@ -148,41 +185,14 @@
         ]
         ct[quad] = jnp.concatenate(rows, axis=0).T.astype(BF16)
 
-    load_f.wait()
-    pl.semaphore_wait(barrier, len(greeted))
-    pl.semaphore_signal(token, inc=1, device_id=across, device_id_type=MESH)
-
-    later(raw.at[pl.ds(0, ZL - 1)], zs_sem)
-    later(raw.at[pl.ds(0, ZL * (Y - 1))], ys_sem)
-
-    def piece(q, block):
-        return raw.at[block, pl.ds(q * ROWS, ROWS)]
-
-    def along_y(q, block, far):
-        part = piece(q, block)
-        for peer in y_peers:
-            remote(part, part, ys_sem, yr_sem.at[q, far], at_cells(peer, zl)).start()
-
-    def along_z(q, block, m, slot):
-        part = piece(q, block)
-        remote(
-            part, part, zs_sem, zr_sem.at[q, slot - 1], at_cells(y, z_peer[m])
-        ).start()
-
-    def from_z(q, m):
-        block = y * ZL + z_peer[m]
-        part = piece(q, block)
-        remote(part, part, zs_sem, zr_sem.at[q, m - 1], opposite).wait_recv()
-        return block
-
-    for q in range(CHUNKS):
-        along_z(q, cell, 4, 4)
-    for q in range(CHUNKS):
-        for m in (1, 2, 3):
-            along_z(q, cell, m, m)
-        along_y(q, cell, 0)
-
-    loads[4].wait()
+    for q in range(CHUNKS):
+        for m in (1, 4, 2, 3):
+            block = from_z(q, m)
+            if m == 4:
+                for near in (1, 2, 3):
+                    along_z(q, block, near, near + 4)
+            along_y(q, block, m // 4)
+    loads[5].wait()
     targets = g3[...].reshape(4 * TARGETS, COLS)
     offset = iota((TARGETS, 4 * TARGETS), 1) - 4 * iota((TARGETS, 4 * TARGETS), 0)
     for k in range(4):
@@ -190,13 +200,6 @@
             (offset == k).astype(F32).astype(BF16), targets
         ).astype(BF16)
 
-    for q in range(CHUNKS):
-        for m in (1, 4, 2, 3):
-            block = from_z(q, m)
-            if m == 4:
-                for near in (1, 2, 3):
-                    along_z(q, block, near, near + 4)
-            along_y(q, block, m // 4)
     for q in range(CHUNKS):
         for m in (5, 6, 7):
             along_y(q, from_z(q, m), 1)
@@ -333,7 +336,7 @@
             jax.ShapeDtypeStruct((416, COLS), BF16),
             jax.ShapeDtypeStruct((8, 128), F32),
         ),
-        in_specs=[hbm] * 4 + [pl.BlockSpec(memory_space=pltpu.SMEM)] + [hbm] * 2,
+        in_specs=[hbm] * 4 + [pl.BlockSpec(memory_space=pl.ANY)] + [hbm] * 2,
         out_specs=(vmem, vmem),
         scratch_shapes=[
             pltpu.VMEM((CELLS, 4 * KC, 128), BF16),
@@ -344,6 +347,7 @@
             pltpu.VMEM((1, 52), F32),
             pltpu.VMEM((1, 128), I32),
             pltpu.VMEM((1, 256), I32),
+            pltpu.SMEM((1, 1), I32),
             pltpu.VMEM((CHUNKS, 1024, 256), F32),
             pltpu.VMEM((2, CHUNKS, 416, 256), BF16),
             pltpu.VMEM((CHUNKS, 2, COLS, 128), F32),
@@ -356,7 +360,7 @@
             pltpu.VMEM((TARGETS, 128), F32),
             pltpu.VMEM((CELLS, 8, 128), BF16),
             pltpu.VMEM((CELLS - 1, 8, 128), BF16),
-            dma((6,)),
+            dma((7,)),
             dma, dma((CHUNKS, ZL - 1)),
             dma, dma((CHUNKS, 2)),
             dma((len(PIECES),)), dma((len(PIECES),)),
@@ -374,7 +378,7 @@
         in_hbm(spatial_cov),
         in_hbm(target_print),
         in_hbm(week_scale.reshape(1, 52)),
-        band_width,
+        band_width.reshape(1, 1),
         in_hbm(sounding_weeks.reshape(1, 128)),
         in_hbm(target_weeks.reshape(1, 256)),
     )

time: 55.5 us -> 55.5 us (level)
  no operation moved by 1% of the time
where the time goes in v7:
time: 55.5 us; the launch traced here: 55.4 us
  Pallas kernels  52.7 us (95%)
  local copies, waits for them, and re-layouts  1.32 us (2%)
  between operations  1.29 us (2%)
    pallas_call x1, Pallas kernels, shards(): pl.pallas_call(kernel, out_shape=(jax.ShapeDtypeStruct((416, COLS), BF16)...  52.7 us
    unnamed x2, local copies, waits for them, and re-layouts  1.32 us

profile of v7, /device:TPU:1, one launch (start us, length us, event | category | flops | bytes accessed | tf_op | source)
XLA Modules:
  0.0 55.4 jit_solution(15182402695501148788)
XLA Ops:
  1.3 52.7 %prior_products.1 = (bf16[416,384]{1,0:T(8,128)(2,1)S(1)}, f32[8,128]{1,0:T(8,128)S(1)}) custom-call(bf16[96,128]{1,0:T(8,128)(2,1)} %bitcast.14, bf16[768,384]{1,0:T(8,128)(2,1)} %c_hbm.1, bf16[256,4,384]{2,1,0:T(4,128)(2,1)} %g_hbm.1, f32[1,52]{1,0:T(1,128)} %bitcast.16, s32[1,1]{1,0:T(1,128)} %bitcast.11.band_hbm, s32[1,128]{1,0:T(1,128)} %bitcast.17, ...), custom_call_target="tpu_custom_call" | custom-call | tf_op jit(solution)/shard_map/prior_products/pallas_call | solution.py:333
  54.0 0.7 %copy.12 = bf16[8,52,384]{2,0,1:T(8,128)(2,1)} copy(bf16[8,52,384]{2,0,1:T(8,128)(2,1)S(1)} %bitcast.12) | data formatting | bytes 638976
  54.8 0.6 %copy.13 = f32[128,8]{0,1:T(8,128)} copy(f32[128,8]{0,1:T(8,128)S(1)} %bitcast.13) | data formatting | bytes 8192

commit v8 on v7

--- a/solution.py
+++ b/solution.py
@@ -56,7 +56,7 @@
     f_hbm, c_hbm, g_hbm, scale_hbm, band_hbm, sw_hbm, tw_hbm,
     hq_ref, pc_ref,
     raw, c_buf, ct, g3, g2, scale_v, sw_v, tw_v, band_s,
-    weights, spread, acc, sum_out, sum_in, z_out, z_in, z_own,
+    weights, acc, sum_out, sum_in, z_out, z_in, z_own,
     flux, pair_x, pair_out, pair_in,
     load_sem, zs_sem, zr_sem, ys_sem, yr_sem, ss_sem, sr_sem,
     hs_sem, hr_sem, gs_sem, gr_sem, ps_sem, pr_sem, token,
@@ -200,19 +200,6 @@
             (offset == k).astype(F32).astype(BF16), targets
         ).astype(BF16)
 
-    for q in range(CHUNKS):
-        for m in (5, 6, 7):
-            along_y(q, from_z(q, m), 1)
-
-    mine = (iota((8, 512), 1) & 127) == iota((8, 512), 0) + snd * 8
-    mine = mine.astype(F32)
-    wide = (source_rows[:52].reshape(52, 1, 512) * mine.reshape(1, 8, 512)).reshape(416, 512)
-    wide_hi = wide.astype(BF16)
-    wide_lo = (wide - wide_hi.astype(F32)).astype(BF16)
-    for q in range(CHUNKS):
-        spread[0, q] = wide_hi[:, q * 256 : (q + 1) * 256]
-        spread[1, q] = wide_lo[:, q * 256 : (q + 1) * 256]
-
     def unpack(q, quad):
         blocks = [
             raw[pl.ds((g * 2 + quad) * QUAD, QUAD), q * ROWS : (q + 1) * ROWS].astype(F32)
@@ -290,6 +277,8 @@
         return jnp.sum(both.reshape(4, TARGETS, 128), axis=0)
 
     for q in range(CHUNKS):
+        for m in (5, 6, 7):
+            along_y(q, from_z(q, m), 1)
         near_flux(q)
     for q in range(CHUNKS):
         partial_flux(q)
@@ -302,7 +291,6 @@
     pair_x[...] = total.reshape(TARGETS, 128)
     pair_out[...] = total.astype(BF16)
 
-    later(pair_in, ps_sem)
     for d in (2, 1, 3, 0):
         for m in FAR_FIRST + (0,):
             if m or d:
@@ -311,17 +299,25 @@
                     pair_out.at[target], pair_in.at[m * Y + d - 1], ps_sem, pr_sem, (target, snd)
                 ).start()
 
+    mine = (iota((8, 512), 1) & 127) == iota((8, 512), 0) + snd * 8
+    mine = mine.astype(F32)
+    wide = (source_rows[:52].reshape(52, 1, 512) * mine.reshape(1, 8, 512)).reshape(416, 512)
+    wide_hi = wide.astype(BF16)
+    wide_lo = (wide - wide_hi.astype(F32)).astype(BF16)
     hq = jnp.zeros((416, COLS), F32)
     for q in range(CHUNKS):
         columns = whole_flux(q)
-        hq = hq + dot_nt(spread[0, q], columns) + dot_nt(spread[1, q], columns)
+        lanes = slice(q * 256, (q + 1) * 256)
+        hq = hq + dot_nt(wide_hi[:, lanes], columns) + dot_nt(wide_lo[:, lanes], columns)
     hq_ref[...] = hq.astype(BF16)
 
-    remote(pair_in, pair_in, ps_sem, pr_sem, opposite).wait_recv()
+    finish()
+    last = remote(pair_in, pair_in, ps_sem, pr_sem, opposite)
+    last.wait_recv()
     own = pair_x[pl.ds(pl.multiple_of(cell * 8, 8), 8), :]
     pc_ref[...] = own + jnp.sum(pair_in[...].astype(F32), axis=0)
 
-    finish()
+    last.wait_send()
 
 
 def shards(
@@ -349,7 +345,6 @@
             pltpu.VMEM((1, 256), I32),
             pltpu.SMEM((1, 1), I32),
             pltpu.VMEM((CHUNKS, 1024, 256), F32),
-            pltpu.VMEM((2, CHUNKS, 416, 256), BF16),
             pltpu.VMEM((CHUNKS, 2, COLS, 128), F32),
             pltpu.VMEM((CHUNKS, 2, X, SHARD, 128), BF16),
             pltpu.VMEM((len(PIECES), 2 * X - 1, HALF, 128), BF16),

time: 55.5 us -> 56.5 us (1.018)
  Pallas kernels: 52.7 us -> 53.7 us
    pallas_call x1, Pallas kernels: 52.7 us -> 53.7 us  [shards(): pl.pallas_call(kernel, out_shape=(jax.ShapeDtypeStruct((416, COLS), BF16)...]
where the time goes in v8:
time: 56.5 us; the launch traced here: 56.3 us
  Pallas kernels  53.7 us (95%)
  local copies, waits for them, and re-layouts  1.32 us (2%)
  between operations  1.29 us (2%)
    pallas_call x1, Pallas kernels, shards(): pl.pallas_call(kernel, out_shape=(jax.ShapeDtypeStruct((416, COLS), BF16)...  53.7 us
    unnamed x2, local copies, waits for them, and re-layouts  1.32 us

profile of v8, /device:TPU:1, one launch (start us, length us, event | category | flops | bytes accessed | tf_op | source)
XLA Modules:
  0.0 56.3 jit_solution(8541808252310291085)
XLA Ops:
  1.3 53.7 %prior_products.1 = (bf16[416,384]{1,0:T(8,128)(2,1)S(1)}, f32[8,128]{1,0:T(8,128)S(1)}) custom-call(bf16[96,128]{1,0:T(8,128)(2,1)} %bitcast.14, bf16[768,384]{1,0:T(8,128)(2,1)} %c_hbm.1, bf16[256,4,384]{2,1,0:T(4,128)(2,1)} %g_hbm.1, f32[1,52]{1,0:T(1,128)} %bitcast.16, s32[1,1]{1,0:T(1,128)} %bitcast.11.band_hbm, s32[1,128]{1,0:T(1,128)} %bitcast.17, ...), custom_call_target="tpu_custom_call" | custom-call | tf_op jit(solution)/shard_map/prior_products/pallas_call | solution.py:329
  55.0 0.7 %copy.12 = bf16[8,52,384]{2,0,1:T(8,128)(2,1)} copy(bf16[8,52,384]{2,0,1:T(8,128)(2,1)S(1)} %bitcast.12) | data formatting | bytes 638976
  55.7 0.6 %copy.13 = f32[128,8]{0,1:T(8,128)} copy(f32[128,8]{0,1:T(8,128)S(1)} %bitcast.13) | data formatting | bytes 8192

commit v9 on v8

--- a/solution.py
+++ b/solution.py
@@ -279,6 +279,7 @@
     for q in range(CHUNKS):
         for m in (5, 6, 7):
             along_y(q, from_z(q, m), 1)
+    for q in range(CHUNKS):
         near_flux(q)
     for q in range(CHUNKS):
         partial_flux(q)

time: 56.5 us -> 55.5 us (0.982)
  Pallas kernels: 53.7 us -> 52.7 us
    pallas_call x1, Pallas kernels: 53.7 us -> 52.7 us  [shards(): pl.pallas_call(kernel, out_shape=(jax.ShapeDtypeStruct((416, COLS), BF16)...]
where the time goes in v9:
time: 55.5 us; the launch traced here: 55.3 us
  Pallas kernels  52.7 us (95%)
  local copies, waits for them, and re-layouts  1.32 us (2%)
  between operations  1.29 us (2%)
    pallas_call x1, Pallas kernels, shards(): pl.pallas_call(kernel, out_shape=(jax.ShapeDtypeStruct((416, COLS), BF16)...  52.7 us
    unnamed x2, local copies, waits for them, and re-layouts  1.32 us

profile of v9, /device:TPU:1, one launch (start us, length us, event | category | flops | bytes accessed | tf_op | source)
XLA Modules:
  0.0 55.3 jit_solution(10162212713173458081)
XLA Ops:
  1.3 52.7 %prior_products.1 = (bf16[416,384]{1,0:T(8,128)(2,1)S(1)}, f32[8,128]{1,0:T(8,128)S(1)}) custom-call(bf16[96,128]{1,0:T(8,128)(2,1)} %bitcast.14, bf16[768,384]{1,0:T(8,128)(2,1)} %c_hbm.1, bf16[256,4,384]{2,1,0:T(4,128)(2,1)} %g_hbm.1, f32[1,52]{1,0:T(1,128)} %bitcast.16, s32[1,1]{1,0:T(1,128)} %bitcast.11.band_hbm, s32[1,128]{1,0:T(1,128)} %bitcast.17, ...), custom_call_target="tpu_custom_call" | custom-call | tf_op jit(solution)/shard_map/prior_products/pallas_call | solution.py:330
  54.0 0.7 %copy.12 = bf16[8,52,384]{2,0,1:T(8,128)(2,1)} copy(bf16[8,52,384]{2,0,1:T(8,128)(2,1)S(1)} %bitcast.12) | data formatting | bytes 638976
  54.7 0.6 %copy.13 = f32[128,8]{0,1:T(8,128)} copy(f32[128,8]{0,1:T(8,128)S(1)} %bitcast.13) | data formatting | bytes 8192

commit v10 on v7

--- a/solution.py
+++ b/solution.py
@@ -19,7 +19,7 @@
 QUAD = ZL // 2
 GROUP = Y * QUAD * KC
 TARGETS = 256
-AWAY = (1, 3, 2)
+AWAY = (2, 1, 3)
 FAR_FIRST = (7, 6, 5, 4, 3, 2, 1)
 HALF_LINE = (4, 3, 2, 1)
 

time: 55.5 us -> 55.3 us (level)
  no operation moved by 1% of the time
where the time goes in v10:
time: 55.3 us; the launch traced here: 55.2 us
  Pallas kernels  52.6 us (95%)
  local copies, waits for them, and re-layouts  1.32 us (2%)
  between operations  1.29 us (2%)
    pallas_call x1, Pallas kernels, shards(): pl.pallas_call(kernel, out_shape=(jax.ShapeDtypeStruct((416, COLS), BF16)...  52.6 us
    unnamed x2, local copies, waits for them, and re-layouts  1.32 us

profile of v10, /device:TPU:1, one launch (start us, length us, event | category | flops | bytes accessed | tf_op | source)
XLA Modules:
  0.0 55.2 jit_solution(246282951228018764)
XLA Ops:
  1.3 52.6 %prior_products.1 = (bf16[416,384]{1,0:T(8,128)(2,1)S(1)}, f32[8,128]{1,0:T(8,128)S(1)}) custom-call(bf16[96,128]{1,0:T(8,128)(2,1)} %bitcast.14, bf16[768,384]{1,0:T(8,128)(2,1)} %c_hbm.1, bf16[256,4,384]{2,1,0:T(4,128)(2,1)} %g_hbm.1, f32[1,52]{1,0:T(1,128)} %bitcast.16, s32[1,1]{1,0:T(1,128)} %bitcast.11.band_hbm, s32[1,128]{1,0:T(1,128)} %bitcast.17, ...), custom_call_target="tpu_custom_call" | custom-call | tf_op jit(solution)/shard_map/prior_products/pallas_call | solution.py:333
  53.9 0.7 %copy.12 = bf16[8,52,384]{2,0,1:T(8,128)(2,1)} copy(bf16[8,52,384]{2,0,1:T(8,128)(2,1)S(1)} %bitcast.12) | data formatting | bytes 638976
  54.6 0.6 %copy.13 = f32[128,8]{0,1:T(8,128)} copy(f32[128,8]{0,1:T(8,128)S(1)} %bitcast.13) | data formatting | bytes 8192
